TPU v7x, 256 devices: a whole 4x4x8 slice. The times are simulated.
256 devices in a mesh: seq: 64 (over z, y, x_hi), head: 4 (over x_lo, core).
Axes of the slice: x: 4 (x_hi: 2, x_lo: 2; x = x_hi * 2 + x_lo), y: 4, z: 8, core: 2. Of those that a mesh axis runs over, the one named last changes fastest.
Arguments:
- queries: bfloat16 [32768, 2048], P(('seq', 'head')), may hold values from -6 to 6
- key_rows: bfloat16 [32768, 2048], P(('seq', 'head')), may hold values from -6 to 6
- value_rows: bfloat16 [32768, 2048], P(('seq', 'head')), may hold values from -6 to 6
- cotangent: bfloat16 [32768, 2048], P(('seq', 'head')), may hold values from -192 to 192
- cluster_of: int32 [32768], P('seq'), may hold values from 0 to 127, as said below
- order_tokens: int32 [32768], P('seq'), may hold values from 0 to 32767, as said below
Outputs:
- attended: bfloat16 [32768, 2048], P(('seq', 'head'))
- grad_queries: bfloat16 [32768, 2048], P(('seq', 'head'))
- grad_keys: bfloat16 [32768, 2048], P(('seq', 'head'))
- grad_values: bfloat16 [32768, 2048], P(('seq', 'head'))
Inputs may be any that keep to these rules, and one draw needn't show every extreme that they name: `cluster_of`: each of the 128 clusters holds exactly 256 tokens. Cluster c belongs to owner c // 2 along seq; the 512 tokens of one index of seq lie in the clusters of one owner at most 10 times, and exactly 10 times for some index and owner. Each token appears once; the tokens of cluster 0 come first, then those of cluster 1 and so on: cluster_of[order_tokens[p]] = p // 256.
All inputs are finite; a program needn't handle non-finite values.
Results may differ from a plain program's by a relative error of at most 0.0068.
The roundings to bfloat16 on the way count: a program that leaves them out, or rounds other values in their place, can miss the bound.
Values may be sent and summed in bfloat16 or wider, within the bound.
A program may use at most 64 MiB of HBM per device.

v0:
```python
import jax
import jax.numpy as jnp
from jax import lax
from jax.sharding import PartitionSpec as P

DH = 128
CLUSTER = 256


def packed(rows_in, row_index):
    padded = jnp.concatenate([rows_in, jnp.zeros((1, rows_in.shape[1]), rows_in.dtype)], axis=0)
    return jnp.take(padded, row_index, axis=0)


def cluster_mean(rows_in, owned_count):
    summed = jnp.sum(
        rows_in.reshape(owned_count, CLUSTER, rows_in.shape[1]), axis=1, dtype=jnp.float32
    )
    return (summed / CLUSTER).astype(jnp.bfloat16)


def forward_head(
    query_part, key_part, value_part, key_mean_part, value_mean_part, visible, score_scale
):
    owned_count = visible.shape[0]
    rows_total = query_part.shape[0]
    query_cells = query_part.reshape(owned_count, CLUSTER, DH)
    key_cells = key_part.reshape(owned_count, CLUSTER, DH)
    value_cells = value_part.reshape(owned_count, CLUSTER, DH)
    inner = (
        jnp.einsum("cid,cjd->cij", query_cells, key_cells, preferred_element_type=jnp.float32)
        * score_scale
    )
    outer = (
        jnp.einsum("pd,nd->pn", query_part, key_mean_part, preferred_element_type=jnp.float32)
        * score_scale
    )
    row_top = jnp.maximum(
        jnp.max(jnp.where(visible, inner, -jnp.inf), axis=-1),
        jnp.max(outer, axis=-1).reshape(owned_count, CLUSTER),
    )
    inner_exp = jnp.where(visible, jnp.exp(inner - row_top[..., None]), 0.0)
    outer_exp = jnp.exp(outer - row_top.reshape(rows_total)[:, None])
    row_total = jnp.sum(inner_exp, axis=-1) + jnp.sum(outer_exp, axis=-1).reshape(
        owned_count, CLUSTER
    )
    inner_weight = inner_exp / row_total[..., None]
    outer_weight = outer_exp / row_total.reshape(rows_total)[:, None]
    inner_round = inner_weight.astype(jnp.bfloat16)
    outer_round = outer_weight.astype(jnp.bfloat16)
    mixed = jnp.einsum(
        "cij,cjd->cid", inner_round, value_cells, preferred_element_type=jnp.float32
    ).reshape(rows_total, DH)
    mixed = mixed + jnp.dot(outer_round, value_mean_part, preferred_element_type=jnp.float32)
    return (mixed.astype(jnp.bfloat16), inner_weight, outer_weight, inner_round, outer_round)


def backward_head(
    query_part, key_part, value_part, grad_part, key_mean_part, value_mean_part, cached, score_scale
):
    unused, inner_weight, outer_weight, inner_round, outer_round = cached
    owned_count = inner_weight.shape[0]
    rows_total = query_part.shape[0]
    query_cells = query_part.reshape(owned_count, CLUSTER, DH)
    key_cells = key_part.reshape(owned_count, CLUSTER, DH)
    value_cells = value_part.reshape(owned_count, CLUSTER, DH)
    grad_cells = grad_part.reshape(owned_count, CLUSTER, DH)
    inner_grad = jnp.einsum(
        "cid,cjd->cij", grad_cells, value_cells, preferred_element_type=jnp.float32
    )
    outer_grad = jnp.einsum(
        "pd,nd->pn", grad_part, value_mean_part, preferred_element_type=jnp.float32
    )
    row_delta = jnp.sum(inner_weight * inner_grad, axis=-1)
    row_delta = row_delta + jnp.sum(outer_weight * outer_grad, axis=-1).reshape(
        owned_count, CLUSTER
    )
    inner_step = (inner_weight * (inner_grad - row_delta[..., None])).astype(jnp.bfloat16)
    outer_step = (outer_weight * (outer_grad - row_delta.reshape(rows_total)[:, None])).astype(
        jnp.bfloat16
    )
    grad_query = jnp.einsum(
        "cij,cjd->cid", inner_step, key_cells, preferred_element_type=jnp.float32
    ).reshape(rows_total, DH)
    grad_query = score_scale * (
        grad_query + jnp.dot(outer_step, key_mean_part, preferred_element_type=jnp.float32)
    )
    grad_key_inner = score_scale * jnp.einsum(
        "cij,cid->cjd", inner_step, query_cells, preferred_element_type=jnp.float32
    )
    grad_value_inner = jnp.einsum(
        "cij,cid->cjd", inner_round, grad_cells, preferred_element_type=jnp.float32
    )
    key_mean_grad = score_scale * jnp.einsum(
        "pn,pd->nd", outer_step, query_part, preferred_element_type=jnp.float32
    )
    value_mean_grad = jnp.einsum(
        "pn,pd->nd", outer_round, grad_part, preferred_element_type=jnp.float32
    )
    return (
        grad_query.astype(jnp.bfloat16),
        grad_key_inner,
        grad_value_inner,
        key_mean_grad,
        value_mean_grad,
    )


def per_device(queries, key_rows, value_rows, cotangent, cluster_of, order_tokens):
    seq_count = lax.axis_size("seq")
    head_count = lax.axis_size("head")
    group_rows = cluster_of.shape[0]
    local_width = queries.shape[1] // head_count
    heads_local = local_width // DH
    owned_count = group_rows // CLUSTER
    mean_count = group_rows // seq_count
    capacity = mean_count + mean_count // 4
    score_scale = DH ** (-0.5)
    row_numbers = jnp.arange(group_rows, dtype=jnp.int32)
    anchor = order_tokens // group_rows
    owner_numbers = jnp.arange(seq_count, dtype=jnp.int32)
    home_q, home_k, home_v, home_g = (
        lax.all_to_all(queries, "head", split_axis=1, concat_axis=0, tiled=True),
        lax.all_to_all(key_rows, "head", split_axis=1, concat_axis=0, tiled=True),
        lax.all_to_all(value_rows, "head", split_axis=1, concat_axis=0, tiled=True),
        lax.all_to_all(cotangent, "head", split_axis=1, concat_axis=0, tiled=True),
    )
    target = cluster_of // owned_count
    dest_hits = (target[:, None] == owner_numbers[None, :]).astype(jnp.int32)
    placed = jnp.sum((jnp.cumsum(dest_hits, axis=0) - dest_hits) * dest_hits, axis=1)
    send_slot = target * capacity + placed
    send_index = (
        jnp.full((seq_count * capacity,), group_rows, jnp.int32).at[send_slot].set(row_numbers)
    )
    earlier = (anchor[:, None] == anchor[None, :]) & (order_tokens[None, :] < order_tokens[:, None])
    arrival = anchor * capacity + jnp.sum(earlier, axis=1, dtype=jnp.int32)
    back_index = (
        jnp.full((seq_count * capacity,), group_rows, jnp.int32).at[arrival].set(row_numbers)
    )
    arrived = (
        lax.all_to_all(packed(home_q, send_index), "seq", split_axis=0, concat_axis=0, tiled=True),
        lax.all_to_all(packed(home_k, send_index), "seq", split_axis=0, concat_axis=0, tiled=True),
        lax.all_to_all(packed(home_v, send_index), "seq", split_axis=0, concat_axis=0, tiled=True),
        lax.all_to_all(packed(home_g, send_index), "seq", split_axis=0, concat_axis=0, tiled=True),
    )
    owner_q = jnp.take(arrived[0], arrival, axis=0)
    owner_k = jnp.take(arrived[1], arrival, axis=0)
    owner_v = jnp.take(arrived[2], arrival, axis=0)
    owner_g = jnp.take(arrived[3], arrival, axis=0)
    key_means, value_means = (
        lax.all_gather(cluster_mean(owner_k, owned_count), "seq", axis=0, tiled=True),
        lax.all_gather(cluster_mean(owner_v, owned_count), "seq", axis=0, tiled=True),
    )
    slot_tokens = order_tokens.reshape(owned_count, CLUSTER)
    visible = slot_tokens[:, None, :] <= slot_tokens[:, :, None]
    cached = []
    for head_index in range(heads_local):
        lower, upper = (head_index * DH, (head_index + 1) * DH)
        cached.append(
            forward_head(
                owner_q[:, lower:upper],
                owner_k[:, lower:upper],
                owner_v[:, lower:upper],
                key_means[:, lower:upper],
                value_means[:, lower:upper],
                visible,
                score_scale,
            )
        )
    attended_owner = jnp.concatenate([entry[0] for entry in cached], axis=1)
    pieces = []
    for head_index in range(heads_local):
        lower, upper = (head_index * DH, (head_index + 1) * DH)
        pieces.append(
            backward_head(
                owner_q[:, lower:upper],
                owner_k[:, lower:upper],
                owner_v[:, lower:upper],
                owner_g[:, lower:upper],
                key_means[:, lower:upper],
                value_means[:, lower:upper],
                cached[head_index],
                score_scale,
            )
        )
    grad_q_owner = jnp.concatenate([entry[0] for entry in pieces], axis=1)
    inner_keys = jnp.concatenate([entry[1] for entry in pieces], axis=-1)
    inner_values = jnp.concatenate([entry[2] for entry in pieces], axis=-1)
    mean_key_grads = jnp.concatenate([entry[3] for entry in pieces], axis=1)
    mean_value_grads = jnp.concatenate([entry[4] for entry in pieces], axis=1)
    own_key_grads, own_value_grads = (
        lax.psum_scatter(mean_key_grads, "seq", scatter_dimension=0, tiled=True),
        lax.psum_scatter(mean_value_grads, "seq", scatter_dimension=0, tiled=True),
    )
    grad_k_owner = (
        (inner_keys + (own_key_grads / CLUSTER)[:, None, :])
        .reshape(group_rows, local_width)
        .astype(jnp.bfloat16)
    )
    grad_v_owner = (
        (inner_values + (own_value_grads / CLUSTER)[:, None, :])
        .reshape(group_rows, local_width)
        .astype(jnp.bfloat16)
    )
    results = (
        lax.all_to_all(
            packed(attended_owner, back_index), "seq", split_axis=0, concat_axis=0, tiled=True
        ),
        lax.all_to_all(
            packed(grad_q_owner, back_index), "seq", split_axis=0, concat_axis=0, tiled=True
        ),
        lax.all_to_all(
            packed(grad_k_owner, back_index), "seq", split_axis=0, concat_axis=0, tiled=True
        ),
        lax.all_to_all(
            packed(grad_v_owner, back_index), "seq", split_axis=0, concat_axis=0, tiled=True
        ),
    )
    attended, grad_queries, grad_keys, grad_values = (
        lax.all_to_all(
            jnp.take(results[0], send_slot, axis=0), "head", split_axis=0, concat_axis=1, tiled=True
        ),
        lax.all_to_all(
            jnp.take(results[1], send_slot, axis=0), "head", split_axis=0, concat_axis=1, tiled=True
        ),
        lax.all_to_all(
            jnp.take(results[2], send_slot, axis=0), "head", split_axis=0, concat_axis=1, tiled=True
        ),
        lax.all_to_all(
            jnp.take(results[3], send_slot, axis=0), "head", split_axis=0, concat_axis=1, tiled=True
        ),
    )
    return (attended, grad_queries, grad_keys, grad_values)


def solution(mesh):
    in_specs = (
        P(("seq", "head"), None),
        P(("seq", "head"), None),
        P(("seq", "head"), None),
        P(("seq", "head"), None),
        P("seq"),
        P("seq"),
    )
    out_specs = (
        P(("seq", "head"), None),
        P(("seq", "head"), None),
        P(("seq", "head"), None),
        P(("seq", "head"), None),
    )
    return jax.shard_map(
        per_device, mesh=mesh, in_specs=in_specs, out_specs=out_specs, check_vma=False
    )
```

profile of v0, /device:TPU:1, one launch (start us, length us, event | category | flops | bytes accessed | tf_op | source)
XLA Modules:
  0.0 1574.5 jit_solution(9881383772002847103)
XLA Ops:
  7.2 1.9 copy.174
  9.0 6.8 all-to-all-start.8
  17.9 5.9 all-to-all-done.8
  23.8 4.3 all-to-all-start.2
  29.4 6.7 all-to-all-done.2
  36.1 4.4 all-to-all-start.4
  42.4 2.4 scatter_custom_fusion
  44.9 3.7 all-to-all-done.4
  48.6 4.3 all-to-all-start
  53.0 2.8 gather_fusion.8
  55.8 2.8 gather_fusion.2
  58.6 2.8 gather_fusion.4
  63.3 2.8 gather_fusion
  66.1 1.6 broadcast_select_fusion.4
  67.7 2.1 all_to_all.208
  69.8 12.7 all-to-all-start.9
  83.7 26.6 %all-to-all-done.9 = bf16[64,10,512]{2,1,0:T(8,128)(2,1)S(1)} async-done(((bf16[64,10,512]{2,1,0:T(8,128)(2,1)}), bf16[64,10,512]{2,1,0:T(8,128)(2,1)S(1)}, u32[]{:S(2)}, u32[]{:S(2)}) %all-to-all-start.9) | async-done | bytes 655392 | tf_op jit(solution)/shard_map/all_to_all | solution.py:144
  110.3 7.8 all-to-all-start.1
  118.1 2.1 all_to_all.187
  120.3 25.0 %all-to-all-done.1 = bf16[64,10,512]{2,1,0:T(8,128)(2,1)S(1)} async-done(((bf16[64,10,512]{2,1,0:T(8,128)(2,1)}), bf16[64,10,512]{2,1,0:T(8,128)(2,1)S(1)}, u32[]{:S(2)}, u32[]{:S(2)}) %all-to-all-start.1) | async-done | bytes 655392 | tf_op jit(solution)/shard_map/all_to_all | solution.py:141
  145.3 8.4 all-to-all-start.3
  154.9 25.5 %all-to-all-done.3 = bf16[64,10,512]{2,1,0:T(8,128)(2,1)} async-done(((bf16[64,10,512]{2,1,0:T(8,128)(2,1)}), bf16[64,10,512]{2,1,0:T(8,128)(2,1)}, u32[]{:S(2)}, u32[]{:S(2)}) %all-to-all-start.3) | async-done | bytes 655392 | tf_op jit(solution)/shard_map/all_to_all | solution.py:142
  180.4 8.6 all-to-all-start.5
  192.5 2.4 scatter_custom_fusion.1
  195.8 2.0 gather_fusion.9
  198.0 2.0 gather_fusion.1
  201.4 2.0 gather_fusion.3
  203.4 11.9 all-to-all-done.5
  216.7 2.0 gather_fusion.5
  218.7 1.7 convert_reduce_fusion.1
  220.4 148.8 %all-gather = bf16[64,2,512]{2,1,0:T(2,128)(2,1)S(1)} all-gather(bf16[1,2,512]{2,1,0:T(2,128)(2,1)S(1)} %fusion.88), channel_id=1, replica_groups=mesh['seq'=64,'head'=4] {'seq'}, dimensions={0}, use_global_device_ids=true | all-gather | bytes 133120 | tf_op jit(solution)/shard_map/all_gather | solution.py:151
  384.9 158.5 %all-gather.1 = bf16[64,2,512]{2,1,0:T(2,128)(2,1)} all-gather(bf16[1,2,512]{2,1,0:T(2,128)(2,1)S(1)} %fusion.89), channel_id=1, replica_groups=mesh['seq'=64,'head'=4] {'seq'}, dimensions={0}, use_global_device_ids=true | all-gather | bytes 133120 | tf_op jit(solution)/shard_map/all_gather | solution.py:152
  543.4 1.6 reshape.592
  545.0 1.8 fusion.54
  557.1 2.4 multiply_reduce_fusion.6
  559.5 1.8 fusion.60
  566.4 2.4 multiply_reduce_fusion.7
  568.8 1.8 fusion.63
  584.4 2.5 multiply_reduce_fusion.3
  624.1 3.0 gather_fusion.10
  627.2 2.8 gather_fusion.6
  631.4 697.1 %all-reduce.13.cloned.1.call-done = (f32[128,512]{0,1:T(8,128)}, f32[128,512]{0,1:T(8,128)}) async-done(((f32[128,512]{0,1:T(8,128)}, f32[128,512]{0,1:T(8,128)}), (f32[128,512]{0,1:T(8,128)}, f32[128,512]{0,1:T(8,128)})) %all-reduce.13.cloned.1.call-update) | async-done | bytes 524304
  1330.7 2.8 gather_fusion.14
  1335.7 3.3 gather_fusion.12
  1339.0 2.7 broadcast_select_fusion
  1341.6 2.1 all_to_all.225
  1343.8 9.9 all-to-all-start.14
  1354.8 18.4 %all-to-all-done.14 = bf16[64,10,512]{2,1,0:T(8,128)(2,1)S(1)} async-done(((bf16[64,10,512]{2,1,0:T(8,128)(2,1)}), bf16[64,10,512]{2,1,0:T(8,128)(2,1)S(1)}, u32[]{:S(2)}, u32[]{:S(2)}) %all-to-all-start.14) | async-done | bytes 655392 | tf_op jit(solution)/shard_map/all_to_all | solution.py:215
  1373.2 5.4 all-to-all-start.10
  1378.6 2.1 all_to_all.218
  1380.7 17.5 %all-to-all-done.10 = bf16[64,10,512]{2,1,0:T(8,128)(2,1)S(1)} async-done(((bf16[64,10,512]{2,1,0:T(8,128)(2,1)}), bf16[64,10,512]{2,1,0:T(8,128)(2,1)S(1)}, u32[]{:S(2)}, u32[]{:S(2)}) %all-to-all-start.10) | async-done | bytes 655392 | tf_op jit(solution)/shard_map/all_to_all | solution.py:209
  1398.2 5.7 all-to-all-start.12
  1405.1 24.4 %all-to-all-done.12 = bf16[64,10,512]{2,1,0:T(8,128)(2,1)} async-done(((bf16[64,10,512]{2,1,0:T(8,128)(2,1)}), bf16[64,10,512]{2,1,0:T(8,128)(2,1)}, u32[]{:S(2)}, u32[]{:S(2)}) %all-to-all-start.12) | async-done | bytes 655392 | tf_op jit(solution)/shard_map/all_to_all | solution.py:212
  1429.5 5.9 all-to-all-start.6
  1435.7 2.0 gather_fusion.15
  1437.9 2.0 gather_fusion.11
  1441.3 2.0 gather_fusion.13
  1443.3 19.8 %all-to-all-done.6 = bf16[64,10,512]{2,1,0:T(8,128)(2,1)} async-done(((bf16[64,10,512]{2,1,0:T(8,128)(2,1)}), bf16[64,10,512]{2,1,0:T(8,128)(2,1)}, u32[]{:S(2)}, u32[]{:S(2)}) %all-to-all-start.6) | async-done | bytes 655392 | tf_op jit(solution)/shard_map/all_to_all | solution.py:206
  1464.4 2.0 gather_fusion.7
  1468.1 63.5 %all_to_all.248 = bf16[4,128,512]{2,1,0:T(8,128)(2,1)S(1)} all-to-all(bf16[4,128,512]{2,1,0:T(8,128)(2,1)S(1)} %bitcast.190), channel_id=1, replica_groups=mesh['seq'=64,'head'=4] {'head'}, dimensions={0} | all-to-all | bytes 1048576 | tf_op jit(solution)/shard_map/all_to_all | solution.py:220
  1531.6 11.2 all_to_all.249
  1542.8 11.2 all_to_all.250
  1554.1 4.5 all-to-all-start.15
  1561.1 5.4 all-to-all-done.15
  (516 shorter events, 113.7 us)
Async XLA Ops:
  9.0 6.8 copy-start.32
  9.0 14.8 all-to-all-start.8
  23.8 12.3 all-to-all-start.2
  36.1 4.7 copy-start.34
  36.1 12.4 all-to-all-start.4
  42.4 2.5 copy-start.138
  48.6 12.9 all-to-all-start
  69.8 12.7 copy-start
  69.8 40.5 %all-to-all-start.9 = ((bf16[64,10,512]{2,1,0:T(8,128)(2,1)}), bf16[64,10,512]{2,1,0:T(8,128)(2,1)S(1)}, u32[]{:S(2)}, u32[]{:S(2)}) async-start(bf16[64,10,512]{2,1,0:T(8,128)(2,1)} %all_to_all.208), calls=%async_computation.9 | async-start | bytes 2097152 | tf_op jit(solution)/shard_map/all_to_all | solution.py:144
  110.3 35.0 %all-to-all-start.1 = ((bf16[64,10,512]{2,1,0:T(8,128)(2,1)}), bf16[64,10,512]{2,1,0:T(8,128)(2,1)S(1)}, u32[]{:S(2)}, u32[]{:S(2)}) async-start(bf16[64,10,512]{2,1,0:T(8,128)(2,1)} %all_to_all.180), calls=%async_computation.1 | async-start | bytes 2097152 | tf_op jit(solution)/shard_map/all_to_all | solution.py:141
  145.3 35.1 %all-to-all-start.3 = ((bf16[64,10,512]{2,1,0:T(8,128)(2,1)}), bf16[64,10,512]{2,1,0:T(8,128)(2,1)}, u32[]{:S(2)}, u32[]{:S(2)}) async-start(bf16[64,10,512]{2,1,0:T(8,128)(2,1)} %all_to_all.187), calls=%async_computation.3 | async-start | bytes 2097152 | tf_op jit(solution)/shard_map/all_to_all | solution.py:142
  180.4 34.9 %all-to-all-start.5 = ((bf16[64,10,512]{2,1,0:T(8,128)(2,1)}), bf16[64,10,512]{2,1,0:T(8,128)(2,1)}, u32[]{:S(2)}, u32[]{:S(2)}) async-start(bf16[64,10,512]{2,1,0:T(8,128)(2,1)} %all_to_all.194), calls=%async_computation.5 | async-start | bytes 2097152 | tf_op jit(solution)/shard_map/all_to_all | solution.py:143
  188.9 1139.6 %all-reduce.13.cloned.1.call-start = ((), (), s32[]{:S(2)}) async-start(), calls=%async_computation.16 | async-start | bytes 1048576
  369.4 2.0 copy-start.10
  369.6 2.8 copy-start.80
  370.6 2.5 copy-start.82
  371.4 2.4 copy-start.12
  374.7 1.9 copy-start.30
  375.7 1.5 copy-start.28
  376.0 2.1 copy-start.6
  376.6 1.6 copy-start.106
  378.1 205.5 %copy-start.2 = (f32[2,256,256]{1,2,0:T(8,128)}, f32[2,256,256]{1,2,0:T(8,128)S(1)}, u32[]{:S(2)}) copy-start(f32[2,256,256]{1,2,0:T(8,128)S(1)} %get-tuple-element.69) | copy-start | bytes 1572868
  545.0 1.8 copy-start.11
  545.0 1.8 copy-start.62
  545.0 1.8 copy-start.116
  557.1 2.4 copy-start.122
  559.5 1.8 copy-start.97
  566.4 2.4 copy-start.125
  568.8 1.8 copy-start.87
  568.8 1.8 copy-start.154
  568.8 4.5 copy-start.42
  571.3 4.6 copy-start.135
  584.3 2.6 copy-start.162
  584.3 3.2 copy-start.161
  584.3 3.2 copy-start.160
  584.3 3.2 copy-start.5
  584.4 3.2 copy-start.7
  584.4 3.2 copy-start.136
  587.6 1.6 copy-start.31
  602.8 1.8 copy-start.45
  602.8 1.8 copy-start.117
  604.6 1.6 copy-start.120
  604.7 1.5 copy-start.44
  606.2 1.7 copy-start.71
  606.2 1.7 copy-start.123
  606.3 1.6 copy-start.46
  607.9 1.7 copy-start.75
  607.9 1.7 copy-start.126
  608.0 1.6 copy-start.47
  627.1 2.8 copy-start.35
  627.2 2.8 copy-start.109
  627.2 2.8 copy-start.115
  631.1 698.6 %copy-start.53 = (f32[2,256,128]{2,1,0:T(8,128)S(1)}, f32[2,256,128]{2,1,0:T(8,128)}, u32[]{:S(2)}) copy-start(f32[2,256,128]{2,1,0:T(8,128)} %fusion.37) | copy-start | bytes 786436
  1330.7 2.8 copy-start.43
  1330.7 3.1 copy-start.26
  1330.7 3.1 copy-start.27
  1335.7 3.3 copy-start.163
  1343.8 9.9 copy-start.1
  1343.8 29.4 %all-to-all-start.14 = ((bf16[64,10,512]{2,1,0:T(8,128)(2,1)}), bf16[64,10,512]{2,1,0:T(8,128)(2,1)S(1)}, u32[]{:S(2)}, u32[]{:S(2)}) async-start(bf16[64,10,512]{2,1,0:T(8,128)(2,1)} %all_to_all.225), calls=%async_computation.14 | async-start | bytes 2097152 | tf_op jit(solution)/shard_map/all_to_all | solution.py:215
  1373.2 25.0 %all-to-all-start.10 = ((bf16[64,10,512]{2,1,0:T(8,128)(2,1)}), bf16[64,10,512]{2,1,0:T(8,128)(2,1)S(1)}, u32[]{:S(2)}, u32[]{:S(2)}) async-start(bf16[64,10,512]{2,1,0:T(8,128)(2,1)} %all_to_all.211), calls=%async_computation.10 | async-start | bytes 2097152 | tf_op jit(solution)/shard_map/all_to_all | solution.py:209
  1398.2 31.3 %all-to-all-start.12 = ((bf16[64,10,512]{2,1,0:T(8,128)(2,1)}), bf16[64,10,512]{2,1,0:T(8,128)(2,1)}, u32[]{:S(2)}, u32[]{:S(2)}) async-start(bf16[64,10,512]{2,1,0:T(8,128)(2,1)} %all_to_all.218), calls=%async_computation.12 | async-start | bytes 2097152 | tf_op jit(solution)/shard_map/all_to_all | solution.py:212
  1405.1 30.4 %copy-start.139 = (s32[512]{0:T(512)S(1)}, s32[512]{0:T(512)}, u32[]{:S(2)}) copy-start(s32[512]{0:T(512)} %copy-done.138) | copy-start | bytes 6148
  1429.5 33.5 %all-to-all-start.6 = ((bf16[64,10,512]{2,1,0:T(8,128)(2,1)}), bf16[64,10,512]{2,1,0:T(8,128)(2,1)}, u32[]{:S(2)}, u32[]{:S(2)}) async-start(bf16[64,10,512]{2,1,0:T(8,128)(2,1)} %all_to_all.197), calls=%async_computation.6 | async-start | bytes 2097152 | tf_op jit(solution)/shard_map/all_to_all | solution.py:206
  1554.1 12.5 all-to-all-start.15
  (116 other events, 102.5 us)
Sparse Core Ops, SparseCore 0:
  623.6 704.8 all-reduce.12
where the time goes:
time: 1590 us; the launch traced here: 1570 us
  waiting for transfers between devices  888 us (56%)
  blocking collectives  393 us (25%)
  local copies, waits for them, and re-layouts  123 us (8%)
  starting transfers between devices  89.3 us (6%)
  matrix products  42.5 us (3%)
  other arithmetic  21.9 us (1%)
  between operations  16.6 us (1%)
    unnamed x2, waiting for transfers between devices  697 us
    all_gather x1, blocking collectives, per_device(): lax.all_gather(cluster_mean(owner_v, owned_count), 'seq', axis=0, tiled=T...  158 us
    all_gather x1, blocking collectives, per_device(): lax.all_gather(cluster_mean(owner_k, owned_count), 'seq', axis=0, tiled=T...  149 us
    all_to_all x1, blocking collectives, per_device(): lax.all_to_all(jnp.take(results[0], send_slot, axis=0), 'head', split_axi...  63.5 us
    unnamed x351, local copies, waits for them, and re-layouts  37.7 us
  transfers between devices with their start and end apart: 14, of which 13 were waited for; matrix products, arithmetic and copies ran while one was open for 3% of the time, Pallas kernels for 0%

commit v1 on v0

v1 whole, which is shorter than its diff:
```python
import functools

import jax
import jax.numpy as jnp
from jax import lax
from jax.experimental import pallas as pl
from jax.experimental.pallas import tpu as pltpu
from jax.sharding import PartitionSpec as P

DH = 128
CLUSTER = 256
MESH = pl.DeviceIdType.MESH
F32 = jnp.float32
BF16 = jnp.bfloat16

TILE = 32


def dot(a, b, dims=((1,), (0,))):
    return lax.dot_general(a, b, (dims, ((), ())), preferred_element_type=F32)


def as_column(row):
    return jnp.transpose(jnp.broadcast_to(row, (128, row.shape[1])))[:, :1]


def slot_vectors(group, rank_key, capacity):
    group_col, key_col = as_column(group), as_column(rank_key)
    same = group_col == group
    rank_col = jnp.sum(jnp.where(same & (rank_key < key_col), 1.0, 0.0), axis=1, keepdims=True)
    rank_row = jnp.sum(jnp.where(same & (key_col < rank_key), 1.0, 0.0), axis=0, keepdims=True)
    return group * capacity + rank_row, group_col * capacity + rank_col


def one_hot_rows(slot_row, count):
    slots = lax.broadcasted_iota(jnp.int32, (count, slot_row.shape[1]), 0).astype(F32)
    return jnp.where(slots == slot_row, 1.0, 0.0).astype(BF16)


def one_hot_columns(slot_col, count):
    slots = lax.broadcasted_iota(jnp.int32, (slot_col.shape[0], count), 1).astype(F32)
    return jnp.where(slots == slot_col, 1.0, 0.0).astype(BF16)


def kernel(
    seq_count, head_count, heads, capacity,
    q_ref, k_ref, v_ref, g_ref, cluster_ref, order_ref,
    out_a, out_q, out_k, out_v,
    home, mid, send_buf, recv_buf, owned, mean_msg, mean_buf, means,
    results, inner, mean_acc, grad_msg, grad_buf, grad_sum, back_send, back_recv, home_out,
    spread, gather, unsort, resort, tile_perm, tile_back, hidden,
    home_send, home_recv, there_send, there_recv, mean_send, mean_recv, grad_send, grad_recv,
    back_send_sem, back_recv_sem, out_send, out_recv,
):
    me = lax.axis_index("seq")
    my_head = lax.axis_index("head")
    combos = 2 * heads
    width = heads * DH
    rows = q_ref.shape[0]
    group_rows = rows * head_count
    owned_count = group_rows // CLUSTER
    slots = seq_count * capacity
    block = capacity * combos
    mean_rows = owned_count * combos
    mean_count = seq_count * owned_count
    scale = DH ** (-0.5)
    pairs = combos // 2

    def peer(step):
        return lax.rem(me + step, seq_count)

    def head_peer(step):
        return lax.rem(my_head + step, head_count)

    barrier = pltpu.get_barrier_semaphore()

    @pl.loop(1, head_count)
    def _(step):
        pl.semaphore_signal(
            barrier, inc=1, device_id={"head": head_peer(step)}, device_id_type=MESH
        )

    @pl.loop(1, seq_count)
    def _(step):
        pl.semaphore_signal(barrier, inc=1, device_id={"seq": peer(step)}, device_id_type=MESH)

    pl.semaphore_wait(barrier, head_count - 1 + seq_count - 1)

    def wait_bytes(ref, semaphore):
        pltpu.make_async_copy(ref, ref, semaphore).wait()

    my_rows = pl.ds(pl.multiple_of(my_head * rows, rows), rows)
    my_lanes = pl.ds(pl.multiple_of(my_head * width, width), width)
    arrays = (k_ref, v_ref, q_ref, g_ref)
    for index, ref in enumerate(arrays):
        chunk = index // 2

        @pl.loop(1, head_count)
        def _(step, index=index, ref=ref, chunk=chunk):
            other = head_peer(step)
            pltpu.make_async_remote_copy(
                src_ref=ref.at[:, pl.ds(pl.multiple_of(other * width, width), width)],
                dst_ref=home.at[index, my_rows],
                send_sem=home_send.at[chunk],
                recv_sem=home_recv.at[chunk],
                device_id={"head": other},
                device_id_type=MESH,
            ).start()

        home[index, my_rows, :] = ref[:, my_lanes]

    target = (cluster_ref[...] // owned_count).astype(F32)
    position = lax.broadcasted_iota(jnp.int32, (1, group_rows), 1).astype(F32)
    row, column = slot_vectors(target, position, capacity)
    spread[...] = one_hot_rows(row, slots)
    gather[...] = one_hot_columns(column, slots)
    tokens_int = order_ref[...]
    tokens = tokens_int.astype(F32)
    row, column = slot_vectors((tokens_int // group_rows).astype(F32), tokens, capacity)
    unsort[...] = one_hot_rows(row, slots)
    resort[...] = one_hot_columns(column, slots)
    side = TILE * combos
    first = lax.broadcasted_iota(jnp.int32, (side, side), 0)
    second = lax.broadcasted_iota(jnp.int32, (side, side), 1)
    tile_perm[...] = jnp.where(
        second == (first % combos) * TILE + first // combos, 1.0, 0.0
    ).astype(BF16)
    tile_back[...] = jnp.where(
        first == (second % combos) * TILE + second // combos, 1.0, 0.0
    ).astype(BF16)
    for c in range(owned_count):
        part = tokens[:, c * CLUSTER : (c + 1) * CLUSTER]
        hidden[c] = jnp.where(as_column(part) <= part, 0.0, -jnp.inf)
    if mean_buf.shape[0] > seq_count * mean_rows:
        mean_buf[...] = jnp.zeros_like(mean_buf)

    def pack(one_hot, source, target_ref, chunk):
        for i in range(pairs):
            mid[i] = dot(one_hot[...], source(i)).astype(BF16)

        @pl.loop(0, slots // (2 * TILE))
        def _(g):
            at = pl.multiple_of(g * 2 * TILE, 2 * TILE)
            halves = []
            for half in range(2):
                pieces = []
                for i in range(pairs):
                    piece = mid[i, pl.ds(at + half * TILE, TILE), :]
                    pieces += [piece[:, :DH], piece[:, DH:]]
                halves.append(jnp.concatenate(pieces, axis=0))
            moved = dot(tile_perm[...], jnp.concatenate(halves, axis=1)).astype(BF16)
            to = pl.multiple_of(g * 2 * side, 2 * side)
            target_ref[chunk, pl.ds(to, side), :] = moved[:, :DH]
            target_ref[chunk, pl.ds(to + side, side), :] = moved[:, DH:]

    def unpack(source_ref, chunk, one_hot, sink):
        @pl.loop(0, slots // (2 * TILE))
        def _(g):
            at = pl.multiple_of(g * 2 * TILE, 2 * TILE)
            start = pl.multiple_of(g * 2 * side, 2 * side)
            both = jnp.concatenate(
                [source_ref[chunk, pl.ds(start, side), :], source_ref[chunk, pl.ds(start + side, side), :]],
                axis=1,
            )
            moved = dot(tile_back[...], both).astype(BF16)
            for half in range(2):
                lanes = slice(half * DH, (half + 1) * DH)
                for i in range(pairs):
                    low = moved[2 * i * TILE : (2 * i + 1) * TILE, lanes]
                    high = moved[(2 * i + 1) * TILE : (2 * i + 2) * TILE, lanes]
                    mid[i, pl.ds(at + half * TILE, TILE), :] = jnp.concatenate([low, high], axis=1)

        for i in range(pairs):
            sink(i, dot(one_hot[...], mid[i]).astype(BF16))

    def exchange(source_ref, dest_ref, size, send_sem, recv_sem):
        mine = pl.ds(pl.multiple_of(me * size, size), size)

        @pl.loop(1, seq_count)
        def _(step):
            other = peer(step)
            pltpu.make_async_remote_copy(
                src_ref=source_ref.at[pl.ds(pl.multiple_of(other * size, size), size)],
                dst_ref=dest_ref.at[mine],
                send_sem=send_sem,
                recv_sem=recv_sem,
                device_id={"seq": other},
                device_id_type=MESH,
            ).start()

        dest_ref[mine, :] = source_ref[mine, :]

    def wait_exchange(ref, size, semaphore):
        wait_bytes(ref.at[pl.ds(0, (seq_count - 1) * size)], semaphore)

    others = pl.ds(0, (head_count - 1) * rows)

    def to_owners(chunk):
        if head_count > 1:
            wait_bytes(home.at[pl.ds(2 * chunk, 2), others], home_recv.at[chunk])

        def source(i):
            lane = (i % (pairs // 2)) * 2 * DH
            return home[2 * chunk + i // (pairs // 2), :, lane : lane + 2 * DH]

        pack(spread, source, send_buf, chunk)
        exchange(
            send_buf.at[chunk], recv_buf.at[chunk], block, there_send.at[chunk], there_recv.at[chunk]
        )

    def at_owner(chunk):
        wait_exchange(recv_buf.at[chunk], block, there_recv.at[chunk])

        def sink(i, value):
            owned[chunk * combos + 2 * i] = value[:, :DH]
            owned[chunk * combos + 2 * i + 1] = value[:, DH:]

        unpack(recv_buf, chunk, resort, sink)

    to_owners(0)
    to_owners(1)
    at_owner(0)

    for c in range(owned_count):
        mean_of = [
            jnp.sum(owned[i, c * CLUSTER : (c + 1) * CLUSTER, :].astype(F32), axis=0, keepdims=True)
            for i in range(combos)
        ]
        for i in range(combos):
            mean_msg[c * combos + i : c * combos + i + 1, :] = mean_of[i] / CLUSTER
    my_means = pl.ds(pl.multiple_of(me * mean_rows, mean_rows), mean_rows)
    mean_buf[my_means, :] = mean_msg[...].astype(BF16)

    @pl.loop(1, seq_count)
    def _(step):
        pltpu.make_async_remote_copy(
            src_ref=mean_buf.at[my_means],
            dst_ref=mean_buf.at[my_means],
            send_sem=mean_send,
            recv_sem=mean_recv,
            device_id={"seq": peer(step)},
            device_id_type=MESH,
        ).start()

    at_owner(1)
    wait_exchange(mean_buf, mean_rows, mean_recv)

    for g in range(mean_buf.shape[0] // side):
        moved = dot(tile_back[...], mean_buf[g * side : (g + 1) * side, :]).astype(BF16)
        for i in range(combos):
            means[i, g * TILE : (g + 1) * TILE, :] = moved[i * TILE : (i + 1) * TILE, :]

    @pl.loop(0, heads)
    def _(h):
        key_means = means[h, :mean_count, :]
        value_means = means[heads + h, :mean_count, :]
        for c in range(owned_count):
            part = pl.ds(c * CLUSTER, CLUSTER)
            keys = jnp.concatenate([owned[h, part, :], key_means], axis=0)
            values = jnp.concatenate([owned[heads + h, part, :], value_means], axis=0)
            queries = owned[combos + h, part, :]
            grads = owned[combos + heads + h, part, :]
            scores = dot(keys, queries, ((1,), (1,))) * scale
            scores = jnp.concatenate([scores[:CLUSTER] + hidden[c], scores[CLUSTER:]], axis=0)
            top = jnp.max(scores, axis=0, keepdims=True)
            powers = jnp.exp(scores - top)
            weights = powers * (1.0 / jnp.sum(powers, axis=0, keepdims=True))
            rounded = weights.astype(BF16)
            weight_grads = dot(values, grads, ((1,), (1,)))
            delta = jnp.sum(weights * weight_grads, axis=0, keepdims=True)
            steps = (weights * (weight_grads - delta)).astype(BF16)
            results[h, part, :] = dot(rounded, values, ((0,), (0,))).astype(BF16)
            results[heads + h, part, :] = (scale * dot(steps, keys, ((0,), (0,)))).astype(BF16)
            key_grads = scale * dot(steps, queries)
            value_grads = dot(rounded, grads)
            inner[h, part, :] = key_grads[:CLUSTER]
            inner[heads + h, part, :] = value_grads[:CLUSTER]
            if c == 0:
                mean_acc[h] = key_grads[CLUSTER:]
                mean_acc[heads + h] = value_grads[CLUSTER:]
            else:
                mean_acc[h] += key_grads[CLUSTER:]
                mean_acc[heads + h] += value_grads[CLUSTER:]

    for i in range(combos):
        grad_msg[pl.ds(i, mean_count, stride=combos), :] = mean_acc[i]
    exchange(grad_msg, grad_buf, mean_rows, grad_send, grad_recv)

    def result_pair(i):
        return jnp.concatenate([results[2 * i], results[2 * i + 1]], axis=1)

    pack(unsort, result_pair, back_send, 0)
    exchange(
        back_send.at[0], back_recv.at[0], block, back_send_sem.at[0], back_recv_sem.at[0]
    )

    wait_exchange(grad_buf, mean_rows, grad_recv)
    grad_sum[...] = jnp.sum(grad_buf[...].reshape(seq_count, mean_rows, DH), axis=0) / CLUSTER

    def final_pair(i):
        sides = []
        for j in (2 * i, 2 * i + 1):
            sides.append(
                jnp.concatenate(
                    [
                        inner[j, c * CLUSTER : (c + 1) * CLUSTER, :]
                        + grad_sum[c * combos + j : c * combos + j + 1, :]
                        for c in range(owned_count)
                    ],
                    axis=0,
                )
            )
        return jnp.concatenate(sides, axis=1).astype(BF16)

    pack(unsort, final_pair, back_send, 1)
    exchange(
        back_send.at[1], back_recv.at[1], block, back_send_sem.at[1], back_recv_sem.at[1]
    )

    outs = (out_a, out_q, out_k, out_v)

    def to_home(chunk):
        wait_exchange(back_recv.at[chunk], block, back_recv_sem.at[chunk])

        def sink(i, value):
            lane = (i % (pairs // 2)) * 2 * DH
            home_out[2 * chunk + i // (pairs // 2), :, lane : lane + 2 * DH] = value

        unpack(back_recv, chunk, gather, sink)
        for index in (2 * chunk, 2 * chunk + 1):
            out = outs[index]

            @pl.loop(1, head_count)
            def _(step, index=index, out=out):
                other = head_peer(step)
                pltpu.make_async_remote_copy(
                    src_ref=home_out.at[index, pl.ds(pl.multiple_of(other * rows, rows), rows)],
                    dst_ref=out.at[:, my_lanes],
                    send_sem=out_send.at[chunk],
                    recv_sem=out_recv.at[chunk],
                    device_id={"head": other},
                    device_id_type=MESH,
                ).start()

            out[:, my_lanes] = home_out[index, my_rows, :]

    to_home(0)
    to_home(1)

    if head_count > 1:
        for chunk in range(2):
            both = pl.ds(2 * chunk, 2)
            wait_bytes(home_out.at[both, others], out_recv.at[chunk])
            wait_bytes(home_out.at[both, others], out_send.at[chunk])
            wait_bytes(home.at[both, others], home_send.at[chunk])
    for chunk in range(2):
        wait_exchange(send_buf.at[chunk], block, there_send.at[chunk])
        wait_exchange(back_send.at[chunk], block, back_send_sem.at[chunk])
    wait_exchange(mean_buf, mean_rows, mean_send)
    wait_exchange(grad_msg, mean_rows, grad_send)


def per_device(queries, key_rows, value_rows, cotangent, cluster_of, order_tokens):
    seq_count = lax.axis_size("seq")
    head_count = lax.axis_size("head")
    rows, full = queries.shape
    group_rows = cluster_of.shape[0]
    width = full // head_count
    heads = width // DH
    combos = 2 * heads
    owned_count = group_rows // CLUSTER
    mean_slots = group_rows // seq_count
    capacity = mean_slots + mean_slots // 4
    slots = seq_count * capacity
    side = TILE * combos
    mean_rows = owned_count * combos
    mean_count = seq_count * owned_count
    mean_buf_rows = -(-seq_count * mean_rows // side) * side
    vmem = pltpu.VMEM
    scratch = [
        vmem((4, group_rows, width), BF16),
        vmem((combos // 2, slots, 2 * DH), BF16),
        vmem((2, slots * combos, DH), BF16),
        vmem((2, slots * combos, DH), BF16),
        vmem((2 * combos, group_rows, DH), BF16),
        vmem((mean_rows, DH), F32),
        vmem((mean_buf_rows, DH), BF16),
        vmem((combos, mean_buf_rows // combos, DH), BF16),
        vmem((combos, group_rows, DH), BF16),
        vmem((combos, group_rows, DH), F32),
        vmem((combos, mean_count, DH), F32),
        vmem((seq_count * mean_rows, DH), F32),
        vmem((seq_count * mean_rows, DH), F32),
        vmem((mean_rows, DH), F32),
        vmem((2, slots * combos, DH), BF16),
        vmem((2, slots * combos, DH), BF16),
        vmem((4, group_rows, width), BF16),
        vmem((slots, group_rows), BF16),
        vmem((group_rows, slots), BF16),
        vmem((slots, group_rows), BF16),
        vmem((group_rows, slots), BF16),
        vmem((side, side), BF16),
        vmem((side, side), BF16),
        vmem((owned_count, CLUSTER, CLUSTER), F32),
    ]
    dma = pltpu.SemaphoreType.DMA
    scratch += [dma((2,))] * 4 + [dma] * 4 + [dma((2,))] * 4
    in_vmem = pl.BlockSpec(memory_space=pltpu.VMEM)
    out = jax.ShapeDtypeStruct((rows, full), BF16)
    return pl.pallas_call(
        functools.partial(kernel, seq_count, head_count, heads, capacity),
        out_shape=(out,) * 4,
        in_specs=[in_vmem] * 6,
        out_specs=(in_vmem,) * 4,
        scratch_shapes=scratch,
        compiler_params=pltpu.CompilerParams(
            collective_id=0, has_side_effects=True, vmem_limit_bytes=48 * 1024 * 1024
        ),
    )(
        queries,
        key_rows,
        value_rows,
        cotangent,
        cluster_of.reshape(1, group_rows),
        order_tokens.reshape(1, group_rows),
    )


def solution(mesh):
    rows = P(("seq", "head"), None)
    return jax.shard_map(
        per_device,
        mesh=mesh,
        in_specs=(rows,) * 4 + (P("seq"),) * 2,
        out_specs=(rows,) * 4,
        check_vma=False,
    )
```

time: 1590 us -> 194 us (0.12)
  waiting for transfers between devices: 888 us -> 0 us
  blocking collectives: 393 us -> 0 us
  Pallas kernels: 0 us -> 184 us
  local copies, waits for them, and re-layouts: 123 us -> 8.69 us
  starting transfers between devices: 89.3 us -> 0 us
  matrix products: 42.5 us -> 0 us
  other arithmetic: 21.9 us -> 0 us
  between operations: 16.6 us -> 0.66 us
    unnamed x2 -> x0, waiting for transfers between devices: 697 us -> none
    all_gather x2 -> x0, blocking collectives: 307 us -> none  [the longest x1 158 us: per_device(): lax.all_gather(cluster_mean(owner_v, owned_count), 'seq', axis=0, tiled=T...]
    all_to_all x13 -> x0, waiting for transfers between devices: 191 us -> none  [the longest x1 26.6 us: per_device(): lax.all_to_all(packed(home_g, send_index), 'seq', split_axis=0, concat_ax...]
    pallas_call x0 -> x1, Pallas kernels: none -> 184 us  [per_device(): pl.pallas_call(functools.partial(kernel, seq_count, head_count, heads, ca...]
    all_to_all x13 -> x0, starting transfers between devices: 88.8 us -> none  [the longest x1 12.7 us: per_device(): lax.all_to_all(packed(home_g, send_index), 'seq', split_axis=0, concat_ax...]
    all_to_all x3 -> x0, blocking collectives: 85.9 us -> none  [the longest x1 63.5 us: per_device(): lax.all_to_all(jnp.take(results[0], send_slot, axis=0), 'head', split_axi...]
    dot_general x48 -> x0, matrix products: 42.5 us -> none  [the longest x4 7.66 us: backward_head(): jnp.einsum('pd,nd->pn', grad_part, value_mean_part, preferred_element_typ...]
    gather x16 -> x0, local copies, waits for them, and re-layouts: 38.8 us -> none  [the longest x8 23 us: packed(): return jnp.take(padded, row_index, axis=0)]
  transfers between devices with their start and end apart: 14 -> 0, of which waited for: 13 -> 0; matrix products, arithmetic and copies ran while one was open for 3% -> 0% of each run, Pallas kernels for 0% -> 0%
where the time goes in v1:
time: 194 us
  Pallas kernels  184 us (95%)
  local copies, waits for them, and re-layouts  8.69 us (4%)
    pallas_call x1, Pallas kernels, per_device(): pl.pallas_call(functools.partial(kernel, seq_count, head_count, heads, ca...  184 us
    unnamed x16, local copies, waits for them, and re-layouts  8.69 us

profile of v1, /device:TPU:1, one launch (start us, length us, event | category | flops | bytes accessed | tf_op | source)
XLA Modules:
  0.0 193.6 jit_solution(18443533927188748601)
XLA Ops:
  0.6 0.0 copy-start.4
  0.6 0.7 copy-done.4
  1.3 0.0 copy-start
  1.3 1.0 copy-done
  2.4 0.0 copy-start.1
  2.4 1.0 copy-done.1
  3.4 0.0 copy-start.2
  3.4 1.0 copy-done.2
  4.4 0.0 copy-start.3
  4.4 1.0 copy-done.3
  5.5 0.0 copy-start.5
  5.5 0.7 copy-done.5
  6.2 184.3 %shard_map.93 = (bf16[128,2048]{1,0:T(8,128)(2,1)S(1)}, bf16[128,2048]{1,0:T(8,128)(2,1)S(1)}, bf16[128,2048]{1,0:T(8,128)(2,1)S(1)}, bf16[128,2048]{1,0:T(8,128)(2,1)S(1)}) custom-call(bf16[128,2048]{1,0:T(8,128)(2,1)S(1)} %copy-done, bf16[128,2048]{1,0:T(8,128)(2,1)S(1)} %copy-done.1, bf16[128,2048]{1,0:T(8,128)(2,1)S(1)} %copy-done.2, ...), custom_call_target="tpu_custom_call" | custom-call | tf_op jit(solution)/shard_map/pallas_call | solution.py:410
  190.5 0.8 copy.14
  191.3 0.8 copy.15
  192.1 0.8 copy.16
  192.8 0.8 copy.17
Async XLA Ops:
  0.6 0.7 copy-start.4
  1.3 1.0 copy-start
  2.4 1.0 copy-start.1
  3.4 1.0 copy-start.2
  4.4 1.0 copy-start.3
  5.5 0.7 copy-start.5

commit v2 on v1

v2 whole, which is shorter than its diff:
```python
import functools
import math

import jax
import jax.numpy as jnp
from jax import lax
from jax.experimental import pallas as pl
from jax.experimental.pallas import tpu as pltpu
from jax.sharding import PartitionSpec as P

DH = 128
CLUSTER = 256
MESH = pl.DeviceIdType.MESH
F32 = jnp.float32
BF16 = jnp.bfloat16

TILE = 32


def dot(a, b, dims=((1,), (0,))):
    return lax.dot_general(a, b, (dims, ((), ())), preferred_element_type=F32)


def as_column(row):
    return jnp.transpose(jnp.broadcast_to(row, (128, row.shape[1])))[:, :1]


def slot_vectors(group, rank_key, capacity):
    group_col, key_col = as_column(group), as_column(rank_key)
    same = group_col == group
    rank_col = jnp.sum(jnp.where(same & (rank_key < key_col), 1.0, 0.0), axis=1, keepdims=True)
    rank_row = jnp.sum(jnp.where(same & (key_col < rank_key), 1.0, 0.0), axis=0, keepdims=True)
    return group * capacity + rank_row, group_col * capacity + rank_col


def one_hot_rows(slot_row, count):
    slots = lax.broadcasted_iota(jnp.int32, (count, slot_row.shape[1]), 0).astype(F32)
    return jnp.where(slots == slot_row, 1.0, 0.0).astype(BF16)


def one_hot_columns(slot_col, count):
    slots = lax.broadcasted_iota(jnp.int32, (slot_col.shape[0], count), 1).astype(F32)
    return jnp.where(slots == slot_col, 1.0, 0.0).astype(BF16)


def kernel(
    seq_count, head_count, plane, capacity,
    q_ref, k_ref, v_ref, g_ref, cluster_ref, order_ref,
    out_a, out_q, out_k, out_v,
    home, mid, send_buf, recv_buf, owned, mean_msg, mean_buf, means,
    results, inner, mean_acc, grad_msg, grad_plane, grad_part, grad_line, grad_sum,
    back_send, back_recv, home_out,
    spread, gather, unsort, resort, tile_perm, tile_back, hidden,
    home_own, home_send, home_recv, there_send, there_recv,
    line_send, line_recv, plane_send, plane_recv,
    sum_plane_send, sum_plane_recv, sum_line_send, sum_line_recv,
    back_send_sem, back_recv_sem, out_send, out_recv,
):
    me = lax.axis_index("seq")
    my_head = lax.axis_index("head")
    rows, full = q_ref.shape
    width = full // head_count
    half = width // 2
    combos = 4 * half // DH
    group_rows = rows * head_count
    owned_count = group_rows // CLUSTER
    slots = seq_count * capacity
    block = capacity * combos
    mean_kinds = combos // 2
    mean_rows = owned_count * mean_kinds
    mean_count = seq_count * owned_count
    line = seq_count // plane
    my_line, my_plane = me // plane, lax.rem(me, plane)
    scale = DH ** (-0.5)

    def peer(step):
        return lax.rem(me + step, seq_count)

    def head_peer(step):
        return lax.rem(my_head + step, head_count)

    def line_peer(step):
        return lax.rem(my_line + step, line)

    def plane_peer(step):
        return lax.rem(my_plane + step, plane)

    def stretch(index, size):
        return pl.ds(pl.multiple_of(index * size, size), size)

    barrier = pltpu.get_barrier_semaphore()

    @pl.loop(1, head_count)
    def _(step):
        pl.semaphore_signal(
            barrier, inc=1, device_id={"head": head_peer(step)}, device_id_type=MESH
        )

    @pl.loop(1, seq_count)
    def _(step):
        pl.semaphore_signal(barrier, inc=1, device_id={"seq": peer(step)}, device_id_type=MESH)

    pl.semaphore_wait(barrier, head_count - 1 + seq_count - 1)

    def wait_bytes(ref, semaphore):
        pltpu.make_async_copy(ref, ref, semaphore).wait()

    def send(src, dst, send_sem, recv_sem, device):
        pltpu.make_async_remote_copy(
            src_ref=src,
            dst_ref=dst,
            send_sem=send_sem,
            recv_sem=recv_sem,
            device_id=device,
            device_id_type=MESH,
        ).start()

    my_rows = stretch(my_head, rows)
    others = pl.ds(0, (head_count - 1) * rows)

    def lanes(head, chunk):
        return pl.ds(pl.multiple_of(head * width + chunk * half, half), half)

    def to_heads(chunk):
        for index, ref in enumerate((k_ref, v_ref, q_ref, g_ref)):
            landing = home.at[chunk, index, my_rows]

            @pl.loop(1, head_count)
            def _(step, ref=ref, landing=landing):
                other = head_peer(step)
                send(
                    ref.at[:, lanes(other, chunk)],
                    landing,
                    home_send.at[chunk],
                    home_recv.at[chunk],
                    {"head": other},
                )

            pltpu.make_async_copy(
                ref.at[:, lanes(my_head, chunk)], landing, home_own.at[chunk]
            ).start()

    to_heads(0)

    target = (cluster_ref[...] // owned_count).astype(F32)
    position = lax.broadcasted_iota(jnp.int32, (1, group_rows), 1).astype(F32)
    row, column = slot_vectors(target, position, capacity)
    spread[...] = one_hot_rows(row, slots)
    gather[...] = one_hot_columns(column, slots)
    tokens_int = order_ref[...]
    tokens = tokens_int.astype(F32)
    row, column = slot_vectors((tokens_int // group_rows).astype(F32), tokens, capacity)
    unsort[...] = one_hot_rows(row, slots)
    resort[...] = one_hot_columns(column, slots)
    side = TILE * combos
    first = lax.broadcasted_iota(jnp.int32, (side, side), 0)
    second = lax.broadcasted_iota(jnp.int32, (side, side), 1)
    tile_perm[...] = jnp.where(
        second == (first % combos) * TILE + first // combos, 1.0, 0.0
    ).astype(BF16)
    tile_back[...] = jnp.where(
        first == (second % combos) * TILE + second // combos, 1.0, 0.0
    ).astype(BF16)
    for c in range(owned_count):
        part = tokens[:, c * CLUSTER : (c + 1) * CLUSTER]
        hidden[c] = jnp.where(as_column(part) <= part, 0.0, -jnp.inf)

    def pack(one_hot, source_ref, target_ref):
        @pl.loop(0, 4)
        def _(i):
            mid[i] = dot(one_hot[...], source_ref[i]).astype(BF16)

        @pl.loop(0, slots // (2 * TILE))
        def _(g):
            at = pl.multiple_of(g * 2 * TILE, 2 * TILE)
            parts = []
            for side_by_side in range(2):
                pieces = []
                for i in range(4):
                    piece = mid[i, pl.ds(at + side_by_side * TILE, TILE), :]
                    pieces += [piece[:, lane : lane + DH] for lane in range(0, half, DH)]
                parts.append(jnp.concatenate(pieces, axis=0))
            moved = dot(tile_perm[...], jnp.concatenate(parts, axis=1)).astype(BF16)
            to = pl.multiple_of(g * 2 * side, 2 * side)
            target_ref[pl.ds(to, side), :] = moved[:, :DH]
            target_ref[pl.ds(to + side, side), :] = moved[:, DH:]

    def unpack(source_ref, one_hot, target_ref):
        @pl.loop(0, slots // (2 * TILE))
        def _(g):
            at = pl.multiple_of(g * 2 * TILE, 2 * TILE)
            start = pl.multiple_of(g * 2 * side, 2 * side)
            both = jnp.concatenate(
                [source_ref[pl.ds(start, side), :], source_ref[pl.ds(start + side, side), :]],
                axis=1,
            )
            moved = dot(tile_back[...], both).astype(BF16)
            kinds = half // DH
            for side_by_side in range(2):
                part = moved[:, side_by_side * DH : (side_by_side + 1) * DH]
                for i in range(4):
                    pieces = [
                        part[(i * kinds + j) * TILE : (i * kinds + j + 1) * TILE]
                        for j in range(kinds)
                    ]
                    mid[i, pl.ds(at + side_by_side * TILE, TILE), :] = jnp.concatenate(
                        pieces, axis=1
                    )

        @pl.loop(0, 4)
        def _(i):
            target_ref[i] = dot(one_hot[...], mid[i]).astype(BF16)

    def exchange(source_ref, dest_ref, send_sem, recv_sem):
        mine = stretch(me, block)

        @pl.loop(1, seq_count)
        def _(step):
            other = peer(step)
            send(
                source_ref.at[stretch(other, block)],
                dest_ref.at[mine],
                send_sem,
                recv_sem,
                {"seq": other},
            )

        dest_ref[mine, :] = source_ref[mine, :]

    def wait_exchange(ref, semaphore):
        wait_bytes(ref.at[pl.ds(0, (seq_count - 1) * block)], semaphore)

    def to_owners(chunk):
        if head_count > 1:
            wait_bytes(home.at[chunk, :, others], home_recv.at[chunk])
        wait_bytes(home.at[chunk, :, pl.ds(0, rows)], home_own.at[chunk])
        pack(spread, home.at[chunk], send_buf.at[chunk])
        exchange(
            send_buf.at[chunk], recv_buf.at[chunk], there_send.at[chunk], there_recv.at[chunk]
        )

    def at_owner(chunk):
        wait_exchange(recv_buf.at[chunk], there_recv.at[chunk])
        unpack(recv_buf.at[chunk], resort, owned.at[chunk])

    def mean_gather(chunk):
        buf = mean_buf.at[chunk]
        for c in range(owned_count):
            for i in range(2):
                total = jnp.sum(
                    owned[chunk, i, c * CLUSTER : (c + 1) * CLUSTER, :].astype(F32),
                    axis=0,
                    keepdims=True,
                )
                for j in range(half // DH):
                    at = c * mean_kinds + i * (half // DH) + j
                    mean_msg[at : at + 1, :] = total[:, j * DH : (j + 1) * DH] / CLUSTER
        mine = stretch(my_plane * line + my_line, mean_rows)
        buf[mine, :] = mean_msg[...]

        @pl.loop(1, line)
        def _(step):
            send(
                buf.at[mine],
                buf.at[mine],
                line_send.at[chunk],
                line_recv.at[chunk],
                {"seq": line_peer(step) * plane + my_plane},
            )

        wait_bytes(buf.at[pl.ds(0, (line - 1) * mean_rows)], line_recv.at[chunk])
        my_part = stretch(my_plane, line * mean_rows)

        @pl.loop(1, plane)
        def _(step):
            send(
                buf.at[my_part],
                buf.at[my_part],
                plane_send.at[chunk],
                plane_recv.at[chunk],
                {"seq": my_line * plane + plane_peer(step)},
            )

        wait_bytes(buf.at[pl.ds(0, (plane - 1) * line * mean_rows)], plane_recv.at[chunk])
        for i in range(mean_kinds):
            means[i] = buf[pl.ds(i, mean_count, stride=mean_kinds), :].astype(BF16)

    def attend(chunk):
        kinds = half // DH

        @pl.loop(0, kinds)
        def _(h):
            lane = pl.ds(pl.multiple_of(h * DH, DH), DH)
            key_means = means[h]
            value_means = means[kinds + h]
            for c in range(owned_count):
                part = pl.ds(c * CLUSTER, CLUSTER)
                keys = jnp.concatenate([owned[chunk, 0, part, lane], key_means], axis=0)
                values = jnp.concatenate([owned[chunk, 1, part, lane], value_means], axis=0)
                queries = owned[chunk, 2, part, lane]
                grads = owned[chunk, 3, part, lane]
                scores = dot(keys, queries, ((1,), (1,))) * scale
                scores = jnp.concatenate([scores[:CLUSTER] + hidden[c], scores[CLUSTER:]], axis=0)
                top = jnp.max(scores, axis=0, keepdims=True)
                powers = jnp.exp(scores - top)
                weights = powers * (1.0 / jnp.sum(powers, axis=0, keepdims=True))
                rounded = weights.astype(BF16)
                weight_grads = dot(values, grads, ((1,), (1,)))
                delta = jnp.sum(weights * weight_grads, axis=0, keepdims=True)
                steps = (weights * (weight_grads - delta)).astype(BF16)
                results[0, part, lane] = dot(rounded, values, ((0,), (0,))).astype(BF16)
                results[1, part, lane] = (scale * dot(steps, keys, ((0,), (0,)))).astype(BF16)
                key_grads = scale * dot(steps, queries)
                value_grads = dot(rounded, grads)
                inner[0, part, lane] = key_grads[:CLUSTER]
                inner[1, part, lane] = value_grads[:CLUSTER]
                if c == 0:
                    mean_acc[h] = key_grads[CLUSTER:]
                    mean_acc[kinds + h] = value_grads[CLUSTER:]
                else:
                    mean_acc[h] += key_grads[CLUSTER:]
                    mean_acc[kinds + h] += value_grads[CLUSTER:]

    def grad_reduce(chunk):
        for i in range(mean_kinds):
            grad_msg[chunk, pl.ds(i, mean_count, stride=mean_kinds), :] = mean_acc[i]
        size = line * mean_rows
        mine = stretch(my_plane, size)

        @pl.loop(1, plane)
        def _(step):
            other = plane_peer(step)
            send(
                grad_msg.at[chunk, stretch(other, size)],
                grad_plane.at[chunk, mine],
                sum_plane_send.at[chunk],
                sum_plane_recv.at[chunk],
                {"seq": my_line * plane + other},
            )

        grad_plane[chunk, mine, :] = grad_msg[chunk, mine, :]
        wait_bytes(grad_plane.at[chunk, pl.ds(0, (plane - 1) * size)], sum_plane_recv.at[chunk])
        total = grad_plane[chunk, :size, :]
        for i in range(1, plane):
            total = total + grad_plane[chunk, i * size : (i + 1) * size, :]
        grad_part[chunk] = total
        my_slot = stretch(my_line, mean_rows)

        @pl.loop(1, line)
        def _(step):
            other = line_peer(step)
            send(
                grad_part.at[chunk, stretch(other, mean_rows)],
                grad_line.at[chunk, my_slot],
                sum_line_send.at[chunk],
                sum_line_recv.at[chunk],
                {"seq": other * plane + my_plane},
            )

        grad_line[chunk, my_slot, :] = grad_part[chunk, my_slot, :]
        wait_bytes(grad_line.at[chunk, pl.ds(0, (line - 1) * mean_rows)], sum_line_recv.at[chunk])
        total = grad_line[chunk, :mean_rows, :]
        for i in range(1, line):
            total = total + grad_line[chunk, i * mean_rows : (i + 1) * mean_rows, :]
        grad_sum[...] = total / CLUSTER

    def send_back(chunk):
        kinds = half // DH
        for i in range(2):
            for c in range(owned_count):
                part = slice(c * CLUSTER, (c + 1) * CLUSTER)
                for j in range(kinds):
                    lane = slice(j * DH, (j + 1) * DH)
                    at = c * mean_kinds + i * kinds + j
                    results[2 + i, part, lane] = (
                        inner[i, part, lane] + grad_sum[at : at + 1, :]
                    ).astype(BF16)
        pack(unsort, results, back_send.at[chunk])
        exchange(
            back_send.at[chunk],
            back_recv.at[chunk],
            back_send_sem.at[chunk],
            back_recv_sem.at[chunk],
        )

    def to_home(chunk):
        wait_exchange(back_recv.at[chunk], back_recv_sem.at[chunk])
        unpack(back_recv.at[chunk], gather, home_out.at[chunk])
        for index, out in enumerate((out_a, out_q, out_k, out_v)):

            @pl.loop(1, head_count)
            def _(step, index=index, out=out):
                other = head_peer(step)
                send(
                    home_out.at[chunk, index, stretch(other, rows)],
                    out.at[:, lanes(my_head, chunk)],
                    out_send.at[chunk],
                    out_recv.at[chunk],
                    {"head": other},
                )

            out[:, lanes(my_head, chunk)] = home_out[chunk, index, my_rows, :]

    to_owners(0)
    to_heads(1)
    to_owners(1)
    for chunk in range(2):
        at_owner(chunk)
        mean_gather(chunk)
        attend(chunk)
        grad_reduce(chunk)
        send_back(chunk)
    for chunk in range(2):
        to_home(chunk)

    for chunk in range(2):
        if head_count > 1:
            wait_bytes(home_out.at[chunk, :, others], out_recv.at[chunk])
            wait_bytes(home_out.at[chunk, :, others], out_send.at[chunk])
            wait_bytes(home.at[chunk, :, others], home_send.at[chunk])
        wait_exchange(send_buf.at[chunk], there_send.at[chunk])
        wait_exchange(back_send.at[chunk], back_send_sem.at[chunk])
        line_bytes = mean_buf.at[chunk, pl.ds(0, (line - 1) * mean_rows)]
        plane_bytes = mean_buf.at[chunk, pl.ds(0, (plane - 1) * line * mean_rows)]
        wait_bytes(line_bytes, line_send.at[chunk])
        wait_bytes(plane_bytes, plane_send.at[chunk])
        wait_bytes(plane_bytes, sum_plane_send.at[chunk])
        wait_bytes(line_bytes, sum_line_send.at[chunk])


def per_device(queries, key_rows, value_rows, cotangent, cluster_of, order_tokens):
    seq_count = lax.axis_size("seq")
    head_count = lax.axis_size("head")
    plane = math.isqrt(seq_count)
    rows, full = queries.shape
    group_rows = cluster_of.shape[0]
    width = full // head_count
    half = width // 2
    combos = 4 * half // DH
    owned_count = group_rows // CLUSTER
    mean_slots = group_rows // seq_count
    capacity = mean_slots + mean_slots // 4
    slots = seq_count * capacity
    side = TILE * combos
    mean_kinds = combos // 2
    mean_rows = owned_count * mean_kinds
    mean_count = seq_count * owned_count
    vmem = pltpu.VMEM
    scratch = [
        vmem((2, 4, group_rows, half), BF16),
        vmem((4, slots, half), BF16),
        vmem((2, slots * combos, DH), BF16),
        vmem((2, slots * combos, DH), BF16),
        vmem((2, 4, group_rows, half), BF16),
        vmem((mean_rows, DH), F32),
        vmem((2, seq_count * mean_rows, DH), F32),
        vmem((mean_kinds, mean_count, DH), BF16),
        vmem((4, group_rows, half), BF16),
        vmem((2, group_rows, half), F32),
        vmem((mean_kinds, mean_count, DH), F32),
        vmem((2, seq_count * mean_rows, DH), F32),
        vmem((2, seq_count * mean_rows, DH), F32),
        vmem((2, seq_count // plane * mean_rows, DH), F32),
        vmem((2, seq_count // plane * mean_rows, DH), F32),
        vmem((mean_rows, DH), F32),
        vmem((2, slots * combos, DH), BF16),
        vmem((2, slots * combos, DH), BF16),
        vmem((2, 4, group_rows, half), BF16),
        vmem((slots, group_rows), BF16),
        vmem((group_rows, slots), BF16),
        vmem((slots, group_rows), BF16),
        vmem((group_rows, slots), BF16),
        vmem((side, side), BF16),
        vmem((side, side), BF16),
        vmem((owned_count, CLUSTER, CLUSTER), F32),
    ]
    scratch += [pltpu.SemaphoreType.DMA((2,))] * 17
    anywhere = pl.BlockSpec(memory_space=pl.ANY)
    in_vmem = pl.BlockSpec(memory_space=pltpu.VMEM)
    out = jax.ShapeDtypeStruct((rows, full), BF16)
    return pl.pallas_call(
        functools.partial(kernel, seq_count, head_count, plane, capacity),
        out_shape=(out,) * 4,
        in_specs=[anywhere] * 4 + [in_vmem] * 2,
        out_specs=(in_vmem,) * 4,
        scratch_shapes=scratch,
        compiler_params=pltpu.CompilerParams(
            collective_id=0, has_side_effects=True, vmem_limit_bytes=48 * 1024 * 1024
        ),
    )(
        queries,
        key_rows,
        value_rows,
        cotangent,
        cluster_of.reshape(1, group_rows),
        order_tokens.reshape(1, group_rows),
    )


def solution(mesh):
    rows = P(("seq", "head"), None)
    return jax.shard_map(
        per_device,
        mesh=mesh,
        in_specs=(rows,) * 4 + (P("seq"),) * 2,
        out_specs=(rows,) * 4,
        check_vma=False,
    )
```

time: 194 us -> 218 us (1.12); the launches traced: 194 us -> 215 us
  Pallas kernels: 184 us -> 206 us
    pallas_call x1, Pallas kernels: 184 us -> 206 us  [per_device(): pl.pallas_call(functools.partial(kernel, seq_count, head_count, plane, ca...]
where the time goes in v2:
time: 218 us; the launch traced here: 215 us
  Pallas kernels  206 us (94%)
  local copies, waits for them, and re-layouts  8.69 us (4%)
    pallas_call x1, Pallas kernels, per_device(): pl.pallas_call(functools.partial(kernel, seq_count, head_count, plane, ca...  206 us
    unnamed x16, local copies, waits for them, and re-layouts  8.69 us

profile of v2, /device:TPU:1, one launch (start us, length us, event | category | flops | bytes accessed | tf_op | source)
XLA Modules:
  0.0 214.9 jit_solution(323045402919993669)
XLA Ops:
  0.6 0.0 copy-start.4
  0.6 0.7 copy-done.4
  1.3 0.0 copy-start
  1.3 1.0 copy-done
  2.4 0.0 copy-start.1
  2.4 1.0 copy-done.1
  3.4 0.0 copy-start.2
  3.4 1.0 copy-done.2
  4.4 0.0 copy-start.3
  4.4 1.0 copy-done.3
  5.5 0.0 copy-start.5
  5.5 0.7 copy-done.5
  6.2 205.5 %shard_map.93 = (bf16[128,2048]{1,0:T(8,128)(2,1)S(1)}, bf16[128,2048]{1,0:T(8,128)(2,1)S(1)}, bf16[128,2048]{1,0:T(8,128)(2,1)S(1)}, bf16[128,2048]{1,0:T(8,128)(2,1)S(1)}) custom-call(bf16[128,2048]{1,0:T(8,128)(2,1)S(1)} %copy-done, bf16[128,2048]{1,0:T(8,128)(2,1)S(1)} %copy-done.1, bf16[128,2048]{1,0:T(8,128)(2,1)S(1)} %copy-done.2, ...), custom_call_target="tpu_custom_call" | custom-call | tf_op jit(solution)/shard_map/pallas_call | solution.py:481
  211.7 0.8 copy.14
  212.5 0.8 copy.15
  213.3 0.8 copy.16
  214.1 0.8 copy.17
Async XLA Ops:
  0.6 0.7 copy-start.4
  1.3 1.0 copy-start
  2.4 1.0 copy-start.1
  3.4 1.0 copy-start.2
  4.4 1.0 copy-start.3
  5.5 0.7 copy-start.5

commit v3 on v2

v3 whole, which is shorter than its diff:
```python
import functools
import math

import jax
import jax.numpy as jnp
from jax import lax
from jax.experimental import pallas as pl
from jax.experimental.pallas import tpu as pltpu
from jax.sharding import PartitionSpec as P

DH = 128
CLUSTER = 256
MESH = pl.DeviceIdType.MESH
F32 = jnp.float32
BF16 = jnp.bfloat16

TILE = 32
PARTS = 4


def place_of(index, line, plane):
    at_line, at_plane = index // plane, index % plane
    pair = line // 2
    return (at_line % pair * 2 + at_line // pair) * plane + at_plane


def index_of(place, line, plane):
    at_line, at_plane = place // plane, place % plane
    return (at_line // 2 + at_line % 2 * (line // 2)) * plane + at_plane


def dot(a, b, dims=((1,), (0,))):
    return lax.dot_general(a, b, (dims, ((), ())), preferred_element_type=F32)


def as_column(row):
    return jnp.transpose(jnp.broadcast_to(row, (128, row.shape[1])))[:, :1]


def slot_vectors(group, rank_key, capacity):
    group_col, key_col = as_column(group), as_column(rank_key)
    same = group_col == group
    rank_col = jnp.sum(jnp.where(same & (rank_key < key_col), 1.0, 0.0), axis=1, keepdims=True)
    rank_row = jnp.sum(jnp.where(same & (key_col < rank_key), 1.0, 0.0), axis=0, keepdims=True)
    return group * capacity + rank_row, group_col * capacity + rank_col


def one_hot_rows(slot_row, count):
    slots = lax.broadcasted_iota(jnp.int32, (count, slot_row.shape[1]), 0).astype(F32)
    return jnp.where(slots == slot_row, 1.0, 0.0).astype(BF16)


def one_hot_columns(slot_col, count):
    slots = lax.broadcasted_iota(jnp.int32, (slot_col.shape[0], count), 1).astype(F32)
    return jnp.where(slots == slot_col, 1.0, 0.0).astype(BF16)


def kernel(
    seq_count, head_count, plane, capacity,
    q_ref, k_ref, v_ref, g_ref, cluster_ref, order_ref,
    out_ref,
    cluster_vec, order_vec, home, mid, send_buf, recv_buf, owned, mean_msg, mean_buf, means,
    results, inner, mean_acc, grad_msg, grad_plane, grad_part, grad_line, grad_sum,
    back_send, back_recv, home_out,
    spread, gather, unsort, resort, tile_perm, tile_back, hidden,
    home_own, home_send, home_recv, there_send, there_recv,
    back_send_sem, back_recv_sem, out_send, out_recv,
    table_sem, line_send, line_recv, plane_send, plane_recv,
    sum_plane_send, sum_plane_recv, sum_line_send, sum_line_recv, plane_ready,
):
    me = lax.axis_index("seq")
    my_head = lax.axis_index("head")
    rows, full = q_ref.shape
    width = full // head_count
    half = width // 2
    kinds = half // DH
    combos = 4 * kinds
    heads = width // DH
    group_rows = rows * head_count
    owned_count = group_rows // CLUSTER
    slots = seq_count * capacity
    part_slots = slots // PARTS
    part_peers = seq_count // PARTS
    block = capacity * combos
    side = TILE * combos
    mean_rows = owned_count * combos
    mean_count = seq_count * owned_count
    line = seq_count // plane
    my_line, my_plane = me // plane, lax.rem(me, plane)
    my_place = place_of(me, line, plane)
    my_part = my_place // part_peers
    scale = DH ** (-0.5)

    def head_peer(step):
        return lax.rem(my_head + step, head_count)

    def line_peer(step):
        return lax.rem(my_line + step, line)

    def plane_peer(step):
        return lax.rem(my_plane + step, plane)

    def stretch(index, size):
        return pl.ds(pl.multiple_of(index * size, size), size)

    def wait_bytes(ref, semaphore):
        pltpu.make_async_copy(ref, ref, semaphore).wait()

    def send(src, dst, send_sem, recv_sem, device):
        pltpu.make_async_remote_copy(
            src_ref=src,
            dst_ref=dst,
            send_sem=send_sem,
            recv_sem=recv_sem,
            device_id=device,
            device_id_type=MESH,
        ).start()

    barrier = pltpu.get_barrier_semaphore()

    def greet(semaphore, device):
        pl.semaphore_signal(semaphore, inc=1, device_id=device, device_id_type=MESH)

    @pl.loop(1, head_count)
    def _(step):
        greet(barrier, {"head": head_peer(step)})

    @pl.loop(1, line)
    def _(step):
        greet(barrier, {"seq": line_peer(step) * plane + my_plane})

    @pl.loop(1, plane)
    def _(step):
        greet(barrier, {"seq": my_line * plane + plane_peer(step)})

    table_copies = [
        pltpu.make_async_copy(cluster_ref, cluster_vec, table_sem.at[0]),
        pltpu.make_async_copy(order_ref, order_vec, table_sem.at[1]),
    ]
    for copy in table_copies:
        copy.start()

    pl.semaphore_wait(barrier, head_count - 1 + line - 1 + plane - 1)

    my_rows = stretch(my_head, rows)
    others = pl.ds(0, (head_count - 1) * rows)

    def lanes(head, i):
        return pl.ds(pl.multiple_of(head * width + (i % 2) * half, half), half)

    def to_heads(chunk, pairs=range(4)):
        for i in pairs:
            ref = ((k_ref, v_ref), (q_ref, g_ref))[chunk][i // 2]
            landing = home.at[chunk, i, my_rows]

            @pl.loop(1, head_count)
            def _(step, i=i, ref=ref, landing=landing):
                other = head_peer(step)
                send(
                    ref.at[:, lanes(other, i)],
                    landing,
                    home_send.at[chunk],
                    home_recv.at[chunk],
                    {"head": other},
                )

            pltpu.make_async_copy(
                ref.at[:, lanes(my_head, i)], landing, home_own.at[chunk]
            ).start()

    def from_heads(chunk):
        if head_count > 1:
            wait_bytes(home.at[chunk, :, others], home_recv.at[chunk])
        wait_bytes(home.at[chunk, :, pl.ds(0, rows)], home_own.at[chunk])

    to_heads(0)

    @pl.loop(1, plane)
    def _(step):
        greet(plane_ready, {"seq": my_line * plane + plane_peer(step)})

    for copy in table_copies:
        copy.wait()
    target = place_of(cluster_vec[...] // owned_count, line, plane).astype(F32)
    position = lax.broadcasted_iota(jnp.int32, (1, group_rows), 1).astype(F32)
    row, column = slot_vectors(target, position, capacity)
    spread[...] = one_hot_rows(row, slots)
    gather[...] = one_hot_columns(column, slots)
    tokens_int = order_vec[...]
    tokens = tokens_int.astype(F32)
    source = place_of(tokens_int // group_rows, line, plane).astype(F32)
    row, column = slot_vectors(source, tokens, capacity)
    unsort[...] = one_hot_rows(row, slots)
    resort[...] = one_hot_columns(column, slots)
    first = lax.broadcasted_iota(jnp.int32, (side, side), 0)
    second = lax.broadcasted_iota(jnp.int32, (side, side), 1)
    tile_perm[...] = jnp.where(
        second == (first % combos) * TILE + first // combos, 1.0, 0.0
    ).astype(BF16)
    tile_back[...] = jnp.where(
        first == (second % combos) * TILE + second // combos, 1.0, 0.0
    ).astype(BF16)
    for c in range(owned_count):
        piece = tokens[:, c * CLUSTER : (c + 1) * CLUSTER]
        hidden[c] = jnp.where(as_column(piece) <= piece, 0.0, -jnp.inf)
    if mean_buf.shape[0] > seq_count * mean_rows:
        mean_buf[...] = jnp.zeros_like(mean_buf)

    groups = part_slots // TILE

    def pack_part(one_hot, source_ref, buf, part):
        here = stretch(part, part_slots)
        hot = one_hot[here, :]
        pairs = [dot(hot, source_ref[i]).astype(BF16) for i in range(4)]
        tiles = []
        for g in range(groups):
            pieces = []
            for pair in pairs:
                piece = pair[g * TILE : (g + 1) * TILE]
                pieces += [piece[:, lane : lane + DH] for lane in range(0, half, DH)]
            tiles.append(jnp.concatenate(pieces, axis=0))
        moved = dot(tile_perm[...], jnp.concatenate(tiles, axis=1)).astype(BF16)
        for g in range(groups):
            buf[pl.ds(pl.multiple_of(part * part_slots * combos + g * side, side), side), :] = (
                moved[:, g * DH : (g + 1) * DH]
            )

    def send_part(buf, dest, part, send_sem, recv_sems, extra):
        mine = stretch(my_place, block)

        @pl.loop(0, part_peers)
        def _(step):
            place = part * part_peers + lax.rem(my_place + step * (plane + 1), part_peers)
            other = index_of(place, line, plane)

            @pl.when(place != my_place)
            def _():
                send(
                    buf.at[stretch(place, block)],
                    dest.at[mine],
                    send_sem,
                    recv_sems.at[my_part],
                    {"seq": other},
                )

            @pl.when(place == my_place)
            def _():
                dest[mine, :] = buf[mine, :]

            if extra is not None:
                extra(step)

    def pack_and_send(
        one_hot, source_ref, buf, dest, send_sem, recv_sems, first_step, last_step, extra=None
    ):
        @pl.loop(first_step, last_step)
        def _(step):
            part = lax.rem(my_part + step, PARTS)
            pack_part(one_hot, source_ref, buf, part)
            also = None
            if extra is not None:
                also = lambda inner_step: extra((step - first_step) * part_peers + inner_step)
            send_part(buf, dest, part, send_sem, recv_sems, also)

    def receive(buf, recv_sems):
        @pl.loop(0, PARTS)
        def _(step):
            part = lax.rem(my_part + PARTS - step, PARTS)
            whole = part_peers * block

            @pl.when(part != my_part)
            def _():
                wait_bytes(buf.at[pl.ds(0, whole)], recv_sems.at[part])

            @pl.when(part == my_part)
            def _():
                wait_bytes(buf.at[pl.ds(0, whole - block)], recv_sems.at[part])

            tiles = [
                buf[pl.ds(pl.multiple_of(part * whole + g * side, side), side), :]
                for g in range(groups)
            ]
            moved = dot(tile_back[...], jnp.concatenate(tiles, axis=1)).astype(BF16)
            for g in range(groups):
                column = moved[:, g * DH : (g + 1) * DH]
                to = pl.ds(pl.multiple_of(part * part_slots + g * TILE, TILE), TILE)
                for i in range(4):
                    pieces = [
                        column[(i * kinds + j) * TILE : (i * kinds + j + 1) * TILE]
                        for j in range(kinds)
                    ]
                    mid[i, to, :] = jnp.concatenate(pieces, axis=1)

    def wait_exchange(ref, semaphore):
        wait_bytes(ref.at[pl.ds(0, (seq_count - 1) * block)], semaphore)

    def to_owners(chunk, first_step, last_step):
        pack_and_send(
            spread,
            home.at[chunk],
            send_buf.at[chunk],
            recv_buf.at[chunk],
            there_send.at[chunk],
            there_recv.at[chunk],
            first_step,
            last_step,
        )

    def at_owner(chunk):
        receive(recv_buf.at[chunk], there_recv.at[chunk])

        @pl.loop(0, 4)
        def _(i):
            owned[chunk, i] = dot(resort[...], mid[i]).astype(BF16)

    my_means = stretch(my_plane * line + my_line, mean_rows)

    def mean_line():
        for c in range(owned_count):
            for i in range(4):
                total = jnp.sum(
                    owned[0, i, c * CLUSTER : (c + 1) * CLUSTER, :].astype(F32),
                    axis=0,
                    keepdims=True,
                )
                for j in range(kinds):
                    at = c * combos + i * kinds + j
                    mean_msg[at : at + 1, :] = total[:, j * DH : (j + 1) * DH] / CLUSTER
        mean_buf[my_means, :] = mean_msg[...].astype(BF16)

        @pl.loop(1, line)
        def _(step):
            send(
                mean_buf.at[my_means],
                mean_buf.at[my_means],
                line_send,
                line_recv,
                {"seq": line_peer(step) * plane + my_plane},
            )

    mean_line_bytes = mean_buf.at[pl.ds(0, (line - 1) * mean_rows)]
    mean_plane_bytes = mean_buf.at[pl.ds(0, (plane - 1) * line * mean_rows)]

    def mean_plane():
        wait_bytes(mean_line_bytes, line_recv)
        my_lines = stretch(my_plane, line * mean_rows)

        @pl.loop(1, plane)
        def _(step):
            send(
                mean_buf.at[my_lines],
                mean_buf.at[my_lines],
                plane_send,
                plane_recv,
                {"seq": my_line * plane + plane_peer(step)},
            )

    def mean_take():
        wait_bytes(mean_plane_bytes, plane_recv)
        for g in range(mean_buf.shape[0] // side):
            moved = dot(tile_back[...], mean_buf[g * side : (g + 1) * side, :]).astype(BF16)
            for i in range(combos):
                means[i, g * TILE : (g + 1) * TILE, :] = moved[i * TILE : (i + 1) * TILE, :]

    def attend():
        @pl.loop(0, heads)
        def _(h):
            pair = h // kinds
            lane = pl.ds(pl.multiple_of(lax.rem(h, kinds) * DH, DH), DH)
            key_means = means[h, :mean_count, :]
            value_means = means[heads + h, :mean_count, :]
            for c in range(owned_count):
                part = pl.ds(c * CLUSTER, CLUSTER)
                keys = jnp.concatenate([owned[0, pair, part, lane], key_means], axis=0)
                values = jnp.concatenate([owned[0, 2 + pair, part, lane], value_means], axis=0)
                queries = owned[1, pair, part, lane]
                grads = owned[1, 2 + pair, part, lane]
                scores = dot(keys, queries, ((1,), (1,))) * scale
                scores = jnp.concatenate([scores[:CLUSTER] + hidden[c], scores[CLUSTER:]], axis=0)
                top = jnp.max(scores, axis=0, keepdims=True)
                powers = jnp.exp(scores - top)
                weights = powers * (1.0 / jnp.sum(powers, axis=0, keepdims=True))
                rounded = weights.astype(BF16)
                weight_grads = dot(values, grads, ((1,), (1,)))
                delta = jnp.sum(weights * weight_grads, axis=0, keepdims=True)
                steps = (weights * (weight_grads - delta)).astype(BF16)
                results[pair, part, lane] = dot(rounded, values, ((0,), (0,))).astype(BF16)
                results[2 + pair, part, lane] = (scale * dot(steps, keys, ((0,), (0,)))).astype(
                    BF16
                )
                key_grads = scale * dot(steps, queries)
                value_grads = dot(rounded, grads)
                inner[pair, part, lane] = key_grads[:CLUSTER]
                inner[2 + pair, part, lane] = value_grads[:CLUSTER]
                if c == 0:
                    mean_acc[h] = key_grads[CLUSTER:]
                    mean_acc[heads + h] = value_grads[CLUSTER:]
                else:
                    mean_acc[h] += key_grads[CLUSTER:]
                    mean_acc[heads + h] += value_grads[CLUSTER:]

    plane_size = line * mean_rows

    def grad_pack():
        for i in range(combos):
            grad_msg[pl.ds(i, mean_count, stride=combos), :] = mean_acc[i]
        mine = stretch(my_plane, plane_size)
        grad_plane[mine, :] = grad_msg[mine, :]

    pieces = (plane - 1) * line
    piece_steps = 2 * part_peers
    pieces_per_step = -(-pieces // piece_steps)

    def grad_to_plane(step):
        for i in range(pieces_per_step):
            number = step * pieces_per_step + i

            @pl.when(number < pieces)
            def _(number=number):
                other = plane_peer(number // line + 1)
                at_line = number % line
                send(
                    grad_msg.at[stretch(other * line + at_line, mean_rows)],
                    grad_plane.at[stretch(my_plane * line + at_line, mean_rows)],
                    sum_plane_send,
                    sum_plane_recv,
                    {"seq": my_line * plane + other},
                )

    grad_plane_bytes = grad_plane.at[pl.ds(0, (plane - 1) * plane_size)]
    grad_line_bytes = grad_line.at[pl.ds(0, (line - 1) * mean_rows)]

    def grad_to_line():
        wait_bytes(grad_plane_bytes, sum_plane_recv)
        total = grad_plane[:plane_size, :]
        for i in range(1, plane):
            total = total + grad_plane[i * plane_size : (i + 1) * plane_size, :]
        grad_part[...] = total
        mine = stretch(my_line, mean_rows)

        @pl.loop(1, line)
        def _(step):
            other = line_peer(step)
            send(
                grad_part.at[stretch(other, mean_rows)],
                grad_line.at[mine],
                sum_line_send,
                sum_line_recv,
                {"seq": other * plane + my_plane},
            )

        grad_line[mine, :] = grad_part[mine, :]

    def grad_finish():
        wait_bytes(grad_line_bytes, sum_line_recv)
        total = grad_line[:mean_rows, :]
        for i in range(1, line):
            total = total + grad_line[i * mean_rows : (i + 1) * mean_rows, :]
        grad_sum[...] = total / CLUSTER
        for i in range(4):
            for c in range(owned_count):
                part = slice(c * CLUSTER, (c + 1) * CLUSTER)
                for j in range(kinds):
                    lane = slice(j * DH, (j + 1) * DH)
                    at = c * combos + i * kinds + j
                    results[i, part, lane] = (
                        inner[i, part, lane] + grad_sum[at : at + 1, :]
                    ).astype(BF16)

    def send_back(chunk, first_step, last_step, extra=None):
        pack_and_send(
            unsort,
            results,
            back_send.at[chunk],
            back_recv.at[chunk],
            back_send_sem.at[chunk],
            back_recv_sem.at[chunk],
            first_step,
            last_step,
            extra,
        )

    def to_home(chunk):
        receive(back_recv.at[chunk], back_recv_sem.at[chunk])
        for i in range(4):
            home_out[chunk, i] = dot(gather[...], mid[i]).astype(BF16)
            place = out_ref.at[2 * chunk + i // 2, :, lanes(my_head, i)]

            @pl.loop(1, head_count)
            def _(step, i=i, place=place):
                other = head_peer(step)
                send(
                    home_out.at[chunk, i, stretch(other, rows)],
                    place,
                    out_send.at[chunk],
                    out_recv.at[chunk],
                    {"head": other},
                )

            place[...] = home_out[chunk, i, my_rows, :]

    from_heads(0)
    pl.semaphore_wait(plane_ready, plane - 1)
    to_owners(0, 0, 2)
    to_heads(1, range(2))
    to_owners(0, 2, PARTS)
    to_heads(1, range(2, 4))
    from_heads(1)
    to_owners(1, 0, 2)
    at_owner(0)
    mean_line()
    to_owners(1, 2, 3)
    mean_plane()
    to_owners(1, 3, PARTS)
    mean_take()
    at_owner(1)
    attend()
    grad_pack()
    send_back(0, 0, 2, grad_to_plane)
    send_back(0, 2, 3)
    grad_to_line()
    send_back(0, 3, PARTS)
    grad_finish()
    send_back(1, 0, 2)
    to_home(0)
    send_back(1, 2, PARTS)
    to_home(1)

    for chunk in range(2):
        if head_count > 1:
            wait_bytes(home_out.at[chunk, :, others], out_recv.at[chunk])
            wait_bytes(home_out.at[chunk, :, others], out_send.at[chunk])
            wait_bytes(home.at[chunk, :, others], home_send.at[chunk])
        wait_exchange(send_buf.at[chunk], there_send.at[chunk])
        wait_exchange(back_send.at[chunk], back_send_sem.at[chunk])
    wait_bytes(mean_line_bytes, line_send)
    wait_bytes(mean_plane_bytes, plane_send)
    wait_bytes(grad_plane_bytes, sum_plane_send)
    wait_bytes(grad_line_bytes, sum_line_send)


def per_device(queries, key_rows, value_rows, cotangent, cluster_of, order_tokens):
    seq_count = lax.axis_size("seq")
    head_count = lax.axis_size("head")
    plane = math.isqrt(seq_count)
    rows, full = queries.shape
    group_rows = cluster_of.shape[0]
    width = full // head_count
    half = width // 2
    combos = 4 * half // DH
    owned_count = group_rows // CLUSTER
    mean_slots = group_rows // seq_count
    capacity = mean_slots + mean_slots // 4
    slots = seq_count * capacity
    side = TILE * combos
    mean_rows = owned_count * combos
    mean_count = seq_count * owned_count
    mean_buf_rows = -(-seq_count * mean_rows // side) * side
    line_rows = seq_count // plane * mean_rows
    vmem = pltpu.VMEM
    scratch = [
        vmem((1, group_rows), jnp.int32),
        vmem((1, group_rows), jnp.int32),
        vmem((2, 4, group_rows, half), BF16),
        vmem((4, slots, half), BF16),
        vmem((2, slots * combos, DH), BF16),
        vmem((2, slots * combos, DH), BF16),
        vmem((2, 4, group_rows, half), BF16),
        vmem((mean_rows, DH), F32),
        vmem((mean_buf_rows, DH), BF16),
        vmem((combos, mean_buf_rows // combos, DH), BF16),
        vmem((4, group_rows, half), BF16),
        vmem((4, group_rows, half), F32),
        vmem((combos, mean_count, DH), F32),
        vmem((seq_count * mean_rows, DH), F32),
        vmem((seq_count * mean_rows, DH), F32),
        vmem((line_rows, DH), F32),
        vmem((line_rows, DH), F32),
        vmem((mean_rows, DH), F32),
        vmem((2, slots * combos, DH), BF16),
        vmem((2, slots * combos, DH), BF16),
        vmem((2, 4, group_rows, half), BF16),
        vmem((slots, group_rows), BF16),
        vmem((group_rows, slots), BF16),
        vmem((slots, group_rows), BF16),
        vmem((group_rows, slots), BF16),
        vmem((side, side), BF16),
        vmem((side, side), BF16),
        vmem((owned_count, CLUSTER, CLUSTER), F32),
    ]
    dma = pltpu.SemaphoreType.DMA
    by_chunk, by_part = dma((2,)), dma((2, PARTS))
    scratch += [by_chunk] * 4 + [by_part, by_chunk, by_part] + [by_chunk] * 3 + [dma] * 8
    scratch += [pltpu.SemaphoreType.REGULAR]
    in_hbm = pl.BlockSpec(memory_space=pltpu.HBM)
    in_vmem = pl.BlockSpec(memory_space=pltpu.VMEM)
    staged = pl.pallas_call(
        functools.partial(kernel, seq_count, head_count, plane, capacity),
        out_shape=jax.ShapeDtypeStruct((4, rows, full), BF16),
        in_specs=[in_hbm] * 6,
        out_specs=in_vmem,
        scratch_shapes=scratch,
        compiler_params=pltpu.CompilerParams(
            collective_id=0, has_side_effects=True, vmem_limit_bytes=63 * 1024 * 1024
        ),
    )(
        queries,
        key_rows,
        value_rows,
        cotangent,
        cluster_of.reshape(1, group_rows),
        order_tokens.reshape(1, group_rows),
    )
    return tuple(staged[i] for i in range(4))


def solution(mesh):
    rows = P(("seq", "head"), None)
    return jax.shard_map(
        per_device,
        mesh=mesh,
        in_specs=(rows,) * 4 + (P("seq"),) * 2,
        out_specs=(rows,) * 4,
        check_vma=False,
    )
```

time: 218 us -> 179 us (0.82)
  Pallas kernels: 206 us -> 172 us
  local copies, waits for them, and re-layouts: 8.69 us -> 2.88 us
    pallas_call x1, Pallas kernels: 206 us -> 172 us  [per_device(): pl.pallas_call(functools.partial(kernel, seq_count, head_count, plane, ca...]
    unnamed x16 -> x0, local copies, waits for them, and re-layouts: 8.69 us -> none
    squeeze x0 -> x1, local copies, waits for them, and re-layouts: none -> 2.88 us  [per_device(): return tuple((staged[i] for i in range(4)))]
where the time goes in v3:
time: 179 us; the launch traced here: 176 us
  Pallas kernels  172 us (96%)
  local copies, waits for them, and re-layouts  2.88 us (2%)
    pallas_call x1, Pallas kernels, per_device(): pl.pallas_call(functools.partial(kernel, seq_count, head_count, plane, ca...  172 us

profile of v3, /device:TPU:1, one launch (start us, length us, event | category | flops | bytes accessed | tf_op | source)
XLA Modules:
  0.0 176.0 jit_solution(4063924414015705561)
XLA Ops:
  0.6 172.5 %shard_map.93 = bf16[4,128,2048]{2,1,0:T(8,128)(2,1)} custom-call(bf16[128,2048]{1,0:T(8,128)(2,1)} %q_ref.1, bf16[128,2048]{1,0:T(8,128)(2,1)} %k_ref.1, bf16[128,2048]{1,0:T(8,128)(2,1)} %v_ref.1, bf16[128,2048]{1,0:T(8,128)(2,1)} %g_ref.1, s32[1,512]{1,0:T(1,128)} %bitcast.10, s32[1,512]{1,0:T(1,128)} %bitcast.11), custom_call_target="tpu_custom_call" | custom-call | tf_op jit(solution)/shard_map/pallas_call | solution.py:597
  173.1 2.9 %slice_bitcast_fusion = (bf16[128,2048]{1,0:T(8,128)(2,1)}, bf16[128,2048]{1,0:T(8,128)(2,1)}, bf16[128,2048]{1,0:T(8,128)(2,1)}, bf16[128,2048]{1,0:T(8,128)(2,1)}) fusion(bf16[4,128,2048]{2,1,0:T(8,128)(2,1)} %shard_map.93), kind=kLoop, calls=%fused_computation | loop fusion | bytes 4194304 | tf_op jit(solution)/shard_map/squeeze | solution.py:614

commit v4 on v3

--- a/solution.py
+++ b/solution.py
@@ -37,12 +37,22 @@
     return jnp.transpose(jnp.broadcast_to(row, (128, row.shape[1])))[:, :1]
 
 
-def slot_vectors(group, rank_key, capacity):
+def slot_vectors(group, rank_key, capacity, early, groups):
     group_col, key_col = as_column(group), as_column(rank_key)
     same = group_col == group
     rank_col = jnp.sum(jnp.where(same & (rank_key < key_col), 1.0, 0.0), axis=1, keepdims=True)
     rank_row = jnp.sum(jnp.where(same & (key_col < rank_key), 1.0, 0.0), axis=0, keepdims=True)
-    return group * capacity + rank_row, group_col * capacity + rank_col
+
+    def split(group, rank):
+        late = early * groups + group * (capacity - early) + rank - early
+        return jnp.where(rank < early, group * early + rank, late)
+
+    return (
+        group * capacity + rank_row,
+        group_col * capacity + rank_col,
+        split(group, rank_row),
+        split(group_col, rank_col),
+    )
 
 
 def one_hot_rows(slot_row, count):
@@ -59,10 +69,10 @@
     seq_count, head_count, plane, capacity,
     q_ref, k_ref, v_ref, g_ref, cluster_ref, order_ref,
     out_ref,
-    cluster_vec, order_vec, home, mid, send_buf, recv_buf, owned, mean_msg, mean_buf, means,
-    results, inner, mean_acc, grad_msg, grad_plane, grad_part, grad_line, grad_sum,
+    cluster_vec, order_vec, home, mid, send_buf, recv_buf, owned, asked, mean_msg, mean_buf, means,
+    answers, results, inner, mean_acc, grad_msg, grad_plane, grad_part, grad_line, grad_sum,
     back_send, back_recv, home_out,
-    spread, gather, unsort, resort, tile_perm, tile_back, hidden,
+    spread, gather, spread_split, gather_split, unsort, resort, tile_perm, tile_back, hidden,
     home_own, home_send, home_recv, there_send, there_recv,
     back_send_sem, back_recv_sem, out_send, out_recv,
     table_sem, line_send, line_recv, plane_send, plane_recv,
@@ -79,9 +89,8 @@
     group_rows = rows * head_count
     owned_count = group_rows // CLUSTER
     slots = seq_count * capacity
-    part_slots = slots // PARTS
+    early = capacity * 3 // 5
     part_peers = seq_count // PARTS
-    block = capacity * combos
     side = TILE * combos
     mean_rows = owned_count * combos
     mean_count = seq_count * owned_count
@@ -183,15 +192,30 @@
         copy.wait()
     target = place_of(cluster_vec[...] // owned_count, line, plane).astype(F32)
     position = lax.broadcasted_iota(jnp.int32, (1, group_rows), 1).astype(F32)
-    row, column = slot_vectors(target, position, capacity)
+    row, column, split_row, split_column = slot_vectors(
+        target, position, capacity, early, seq_count
+    )
     spread[...] = one_hot_rows(row, slots)
     gather[...] = one_hot_columns(column, slots)
+    spread_split[...] = one_hot_rows(split_row, slots)
+    gather_split[...] = one_hot_columns(split_column, slots)
     tokens_int = order_vec[...]
     tokens = tokens_int.astype(F32)
     source = place_of(tokens_int // group_rows, line, plane).astype(F32)
-    row, column = slot_vectors(source, tokens, capacity)
+    row, column, _, split_column = slot_vectors(source, tokens, capacity, early, seq_count)
     unsort[...] = one_hot_rows(row, slots)
     resort[...] = one_hot_columns(column, slots)
+    token_column = as_column(tokens)
+    cell_column = (
+        1 + lax.broadcasted_iota(jnp.int32, (group_rows, 1), 0) // CLUSTER
+    ).astype(F32)
+    slot_numbers = lax.broadcasted_iota(jnp.int32, (group_rows, slots), 1).astype(F32)
+    held = slot_numbers == split_column
+    slot_token = jnp.sum(jnp.where(held, token_column, 0.0), axis=0, keepdims=True)
+    slot_cell = jnp.sum(jnp.where(held, cell_column, 0.0), axis=0, keepdims=True)
+    hidden[...] = jnp.where(
+        (cell_column == slot_cell) & (token_column <= slot_token), 0.0, -jnp.inf
+    )
     first = lax.broadcasted_iota(jnp.int32, (side, side), 0)
     second = lax.broadcasted_iota(jnp.int32, (side, side), 1)
     tile_perm[...] = jnp.where(
@@ -200,18 +224,26 @@
     tile_back[...] = jnp.where(
         first == (second % combos) * TILE + second // combos, 1.0, 0.0
     ).astype(BF16)
-    for c in range(owned_count):
-        piece = tokens[:, c * CLUSTER : (c + 1) * CLUSTER]
-        hidden[c] = jnp.where(as_column(piece) <= piece, 0.0, -jnp.inf)
     if mean_buf.shape[0] > seq_count * mean_rows:
         mean_buf[...] = jnp.zeros_like(mean_buf)
 
-    groups = part_slots // TILE
-
-    def pack_part(one_hot, source_ref, buf, part):
-        here = stretch(part, part_slots)
-        hot = one_hot[here, :]
-        pairs = [dot(hot, source_ref[i]).astype(BF16) for i in range(4)]
+    def flow(size, base, one_hot, source_ref, out_buf, in_buf, send_sem, recv_sems):
+        count = size * seq_count
+        here = pl.ds(base * combos, count * combos)
+        return (
+            size, base, one_hot, source_ref, out_buf.at[here], in_buf.at[here], send_sem, recv_sems
+        )
+
+    def pack_part(stream, part):
+        size, base, one_hot, source_ref, buf, _, _, _ = stream
+        part_slots = size * part_peers
+        start = pl.multiple_of(base + part * part_slots, TILE)
+        if one_hot is None:
+            pairs = [source_ref[i, pl.ds(start, part_slots), :] for i in range(4)]
+        else:
+            hot = one_hot[pl.ds(start, part_slots), :]
+            pairs = [dot(hot, source_ref[i]).astype(BF16) for i in range(4)]
+        groups = part_slots // TILE
         tiles = []
         for g in range(groups):
             pieces = []
@@ -225,7 +257,9 @@
                 moved[:, g * DH : (g + 1) * DH]
             )
 
-    def send_part(buf, dest, part, send_sem, recv_sems, extra):
+    def send_part(stream, part, extra):
+        size, _, _, _, buf, dest, send_sem, recv_sems = stream
+        block = size * combos
         mine = stretch(my_place, block)
 
         @pl.loop(0, part_peers)
@@ -250,23 +284,26 @@
             if extra is not None:
                 extra(step)
 
-    def pack_and_send(
-        one_hot, source_ref, buf, dest, send_sem, recv_sems, first_step, last_step, extra=None
-    ):
+    def pack_and_send(stream, first_step, last_step, extra=None):
         @pl.loop(first_step, last_step)
         def _(step):
             part = lax.rem(my_part + step, PARTS)
-            pack_part(one_hot, source_ref, buf, part)
+            pack_part(stream, part)
             also = None
             if extra is not None:
                 also = lambda inner_step: extra((step - first_step) * part_peers + inner_step)
-            send_part(buf, dest, part, send_sem, recv_sems, also)
-
-    def receive(buf, recv_sems):
+            send_part(stream, part, also)
+
+    def receive(stream, target_ref):
+        size, base, _, _, _, buf, _, recv_sems = stream
+        block = size * combos
+        part_slots = size * part_peers
+        groups = part_slots // TILE
+        whole = part_peers * block
+
         @pl.loop(0, PARTS)
         def _(step):
             part = lax.rem(my_part + PARTS - step, PARTS)
-            whole = part_peers * block
 
             @pl.when(part != my_part)
             def _():
@@ -283,35 +320,52 @@
             moved = dot(tile_back[...], jnp.concatenate(tiles, axis=1)).astype(BF16)
             for g in range(groups):
                 column = moved[:, g * DH : (g + 1) * DH]
-                to = pl.ds(pl.multiple_of(part * part_slots + g * TILE, TILE), TILE)
+                to = pl.ds(pl.multiple_of(base + part * part_slots + g * TILE, TILE), TILE)
                 for i in range(4):
                     pieces = [
                         column[(i * kinds + j) * TILE : (i * kinds + j + 1) * TILE]
                         for j in range(kinds)
                     ]
-                    mid[i, to, :] = jnp.concatenate(pieces, axis=1)
-
-    def wait_exchange(ref, semaphore):
-        wait_bytes(ref.at[pl.ds(0, (seq_count - 1) * block)], semaphore)
-
-    def to_owners(chunk, first_step, last_step):
-        pack_and_send(
-            spread,
-            home.at[chunk],
-            send_buf.at[chunk],
-            recv_buf.at[chunk],
-            there_send.at[chunk],
-            there_recv.at[chunk],
-            first_step,
-            last_step,
+                    target_ref[i, to, :] = jnp.concatenate(pieces, axis=1)
+
+    def flows(chunk, one_hot, source_ref, split_hot, split_source, out_buf, in_buf, sends, recvs):
+        first, second = out_buf.at[chunk], in_buf.at[chunk]
+        late = early * seq_count
+        if one_hot is not None:
+            return flow(
+                capacity, 0, one_hot, source_ref, first, second, sends.at[0], recvs.at[0]
+            )
+        return (
+            flow(early, 0, split_hot, split_source, first, second, sends.at[1], recvs.at[1]),
+            flow(
+                capacity - early, late, split_hot, split_source, first, second,
+                sends.at[2], recvs.at[2],
+            ),
         )
 
-    def at_owner(chunk):
-        receive(recv_buf.at[chunk], there_recv.at[chunk])
+    keys_flow = flows(
+        0, spread, home.at[0], None, None, send_buf, recv_buf, there_send, there_recv
+    )
+    query_flows = flows(
+        1, None, None, spread_split, home.at[1], send_buf, recv_buf, there_send, there_recv
+    )
+    answer_flows = flows(
+        0, None, None, None, answers, back_send, back_recv, back_send_sem, back_recv_sem
+    )
+    grads_flow = flows(
+        1, unsort, results, None, None, back_send, back_recv, back_send_sem, back_recv_sem
+    )
+
+    def wait_sent(stream):
+        size, _, _, _, buf, _, send_sem, _ = stream
+        wait_bytes(buf.at[pl.ds(0, (seq_count - 1) * size * combos)], send_sem)
+
+    def keys_arrive():
+        receive(keys_flow, mid)
 
         @pl.loop(0, 4)
         def _(i):
-            owned[chunk, i] = dot(resort[...], mid[i]).astype(BF16)
+            owned[i] = dot(resort[...], mid[i]).astype(BF16)
 
     my_means = stretch(my_plane * line + my_line, mean_rows)
 
@@ -319,7 +373,7 @@
         for c in range(owned_count):
             for i in range(4):
                 total = jnp.sum(
-                    owned[0, i, c * CLUSTER : (c + 1) * CLUSTER, :].astype(F32),
+                    owned[i, c * CLUSTER : (c + 1) * CLUSTER, :].astype(F32),
                     axis=0,
                     keepdims=True,
                 )
@@ -362,42 +416,45 @@
             for i in range(combos):
                 means[i, g * TILE : (g + 1) * TILE, :] = moved[i * TILE : (i + 1) * TILE, :]
 
-    def attend():
+    def attend(which):
+        size, base = query_flows[which][:2]
+        part = pl.ds(base, size * seq_count)
+
         @pl.loop(0, heads)
         def _(h):
             pair = h // kinds
             lane = pl.ds(pl.multiple_of(lax.rem(h, kinds) * DH, DH), DH)
-            key_means = means[h, :mean_count, :]
-            value_means = means[heads + h, :mean_count, :]
-            for c in range(owned_count):
-                part = pl.ds(c * CLUSTER, CLUSTER)
-                keys = jnp.concatenate([owned[0, pair, part, lane], key_means], axis=0)
-                values = jnp.concatenate([owned[0, 2 + pair, part, lane], value_means], axis=0)
-                queries = owned[1, pair, part, lane]
-                grads = owned[1, 2 + pair, part, lane]
-                scores = dot(keys, queries, ((1,), (1,))) * scale
-                scores = jnp.concatenate([scores[:CLUSTER] + hidden[c], scores[CLUSTER:]], axis=0)
-                top = jnp.max(scores, axis=0, keepdims=True)
-                powers = jnp.exp(scores - top)
-                weights = powers * (1.0 / jnp.sum(powers, axis=0, keepdims=True))
-                rounded = weights.astype(BF16)
-                weight_grads = dot(values, grads, ((1,), (1,)))
-                delta = jnp.sum(weights * weight_grads, axis=0, keepdims=True)
-                steps = (weights * (weight_grads - delta)).astype(BF16)
-                results[pair, part, lane] = dot(rounded, values, ((0,), (0,))).astype(BF16)
-                results[2 + pair, part, lane] = (scale * dot(steps, keys, ((0,), (0,)))).astype(
-                    BF16
-                )
-                key_grads = scale * dot(steps, queries)
-                value_grads = dot(rounded, grads)
-                inner[pair, part, lane] = key_grads[:CLUSTER]
-                inner[2 + pair, part, lane] = value_grads[:CLUSTER]
-                if c == 0:
-                    mean_acc[h] = key_grads[CLUSTER:]
-                    mean_acc[heads + h] = value_grads[CLUSTER:]
-                else:
-                    mean_acc[h] += key_grads[CLUSTER:]
-                    mean_acc[heads + h] += value_grads[CLUSTER:]
+            keys = jnp.concatenate([owned[pair, :, lane], means[h, :mean_count, :]], axis=0)
+            values = jnp.concatenate(
+                [owned[2 + pair, :, lane], means[heads + h, :mean_count, :]], axis=0
+            )
+            queries = asked[pair, part, lane]
+            grads = asked[2 + pair, part, lane]
+            scores = dot(keys, queries, ((1,), (1,))) * scale
+            scores = jnp.concatenate(
+                [scores[:group_rows] + hidden[:, part], scores[group_rows:]], axis=0
+            )
+            top = jnp.max(scores, axis=0, keepdims=True)
+            powers = jnp.exp(scores - top)
+            weights = powers * (1.0 / jnp.sum(powers, axis=0, keepdims=True))
+            rounded = weights.astype(BF16)
+            weight_grads = dot(values, grads, ((1,), (1,)))
+            delta = jnp.sum(weights * weight_grads, axis=0, keepdims=True)
+            steps = (weights * (weight_grads - delta)).astype(BF16)
+            answers[pair, part, lane] = dot(rounded, values, ((0,), (0,))).astype(BF16)
+            answers[2 + pair, part, lane] = (scale * dot(steps, keys, ((0,), (0,)))).astype(BF16)
+            key_grads = scale * dot(steps, queries)
+            value_grads = dot(rounded, grads)
+            if which == 0:
+                inner[pair, :, lane] = key_grads[:group_rows]
+                inner[2 + pair, :, lane] = value_grads[:group_rows]
+                mean_acc[h] = key_grads[group_rows:]
+                mean_acc[heads + h] = value_grads[group_rows:]
+            else:
+                inner[pair, :, lane] += key_grads[:group_rows]
+                inner[2 + pair, :, lane] += value_grads[:group_rows]
+                mean_acc[h] += key_grads[group_rows:]
+                mean_acc[heads + h] += value_grads[group_rows:]
 
     plane_size = line * mean_rows
 
@@ -467,23 +524,15 @@
                         inner[i, part, lane] + grad_sum[at : at + 1, :]
                     ).astype(BF16)
 
-    def send_back(chunk, first_step, last_step, extra=None):
-        pack_and_send(
-            unsort,
-            results,
-            back_send.at[chunk],
-            back_recv.at[chunk],
-            back_send_sem.at[chunk],
-            back_recv_sem.at[chunk],
-            first_step,
-            last_step,
-            extra,
-        )
-
     def to_home(chunk):
-        receive(back_recv.at[chunk], back_recv_sem.at[chunk])
+        if chunk == 0:
+            for stream in answer_flows:
+                receive(stream, mid)
+        else:
+            receive(grads_flow, mid)
+        one_hot = (gather_split, gather)[chunk]
         for i in range(4):
-            home_out[chunk, i] = dot(gather[...], mid[i]).astype(BF16)
+            home_out[chunk, i] = dot(one_hot[...], mid[i]).astype(BF16)
             place = out_ref.at[2 * chunk + i // 2, :, lanes(my_head, i)]
 
             @pl.loop(1, head_count)
@@ -501,29 +550,32 @@
 
     from_heads(0)
     pl.semaphore_wait(plane_ready, plane - 1)
-    to_owners(0, 0, 2)
+    pack_and_send(keys_flow, 0, 2)
     to_heads(1, range(2))
-    to_owners(0, 2, PARTS)
+    pack_and_send(keys_flow, 2, PARTS)
     to_heads(1, range(2, 4))
     from_heads(1)
-    to_owners(1, 0, 2)
-    at_owner(0)
+    pack_and_send(query_flows[0], 0, PARTS)
+    keys_arrive()
     mean_line()
-    to_owners(1, 2, 3)
+    pack_and_send(query_flows[1], 0, 2)
     mean_plane()
-    to_owners(1, 3, PARTS)
+    pack_and_send(query_flows[1], 2, PARTS)
     mean_take()
-    at_owner(1)
-    attend()
+    receive(query_flows[0], asked)
+    attend(0)
+    pack_and_send(answer_flows[0], 0, 2)
+    receive(query_flows[1], asked)
+    attend(1)
     grad_pack()
-    send_back(0, 0, 2, grad_to_plane)
-    send_back(0, 2, 3)
+    pack_and_send(answer_flows[0], 2, PARTS, grad_to_plane)
+    pack_and_send(answer_flows[1], 0, 2)
     grad_to_line()
-    send_back(0, 3, PARTS)
+    pack_and_send(answer_flows[1], 2, PARTS)
     grad_finish()
-    send_back(1, 0, 2)
+    pack_and_send(grads_flow, 0, 2)
     to_home(0)
-    send_back(1, 2, PARTS)
+    pack_and_send(grads_flow, 2, PARTS)
     to_home(1)
 
     for chunk in range(2):
@@ -531,8 +583,8 @@
             wait_bytes(home_out.at[chunk, :, others], out_recv.at[chunk])
             wait_bytes(home_out.at[chunk, :, others], out_send.at[chunk])
             wait_bytes(home.at[chunk, :, others], home_send.at[chunk])
-        wait_exchange(send_buf.at[chunk], there_send.at[chunk])
-        wait_exchange(back_send.at[chunk], back_send_sem.at[chunk])
+    for stream in (keys_flow, *query_flows, *answer_flows, grads_flow):
+        wait_sent(stream)
     wait_bytes(mean_line_bytes, line_send)
     wait_bytes(mean_plane_bytes, plane_send)
     wait_bytes(grad_plane_bytes, sum_plane_send)
@@ -565,10 +617,12 @@
         vmem((4, slots, half), BF16),
         vmem((2, slots * combos, DH), BF16),
         vmem((2, slots * combos, DH), BF16),
-        vmem((2, 4, group_rows, half), BF16),
+        vmem((4, group_rows, half), BF16),
+        vmem((4, slots, half), BF16),
         vmem((mean_rows, DH), F32),
         vmem((mean_buf_rows, DH), BF16),
         vmem((combos, mean_buf_rows // combos, DH), BF16),
+        vmem((4, slots, half), BF16),
         vmem((4, group_rows, half), BF16),
         vmem((4, group_rows, half), F32),
         vmem((combos, mean_count, DH), F32),
@@ -584,13 +638,15 @@
         vmem((group_rows, slots), BF16),
         vmem((slots, group_rows), BF16),
         vmem((group_rows, slots), BF16),
+        vmem((slots, group_rows), BF16),
+        vmem((group_rows, slots), BF16),
         vmem((side, side), BF16),
         vmem((side, side), BF16),
-        vmem((owned_count, CLUSTER, CLUSTER), F32),
+        vmem((group_rows, slots), F32),
     ]
     dma = pltpu.SemaphoreType.DMA
-    by_chunk, by_part = dma((2,)), dma((2, PARTS))
-    scratch += [by_chunk] * 4 + [by_part, by_chunk, by_part] + [by_chunk] * 3 + [dma] * 8
+    by_chunk, by_flow, by_part = dma((2,)), dma((3,)), dma((3, PARTS))
+    scratch += [by_chunk] * 3 + [by_flow, by_part] * 2 + [by_chunk] * 3 + [dma] * 8
     scratch += [pltpu.SemaphoreType.REGULAR]
     in_hbm = pl.BlockSpec(memory_space=pltpu.HBM)
     in_vmem = pl.BlockSpec(memory_space=pltpu.VMEM)

time: 179 us -> 172 us (0.961); the launches traced: 176 us -> 172 us
  Pallas kernels: 172 us -> 169 us
    pallas_call x1, Pallas kernels: 172 us -> 169 us  [per_device(): pl.pallas_call(functools.partial(kernel, seq_count, head_count, plane, ca...]
where the time goes in v4:
time: 172 us
  Pallas kernels  169 us (98%)
  local copies, waits for them, and re-layouts  2.88 us (2%)
    pallas_call x1, Pallas kernels, per_device(): pl.pallas_call(functools.partial(kernel, seq_count, head_count, plane, ca...  169 us

profile of v4, /device:TPU:1, one launch (start us, length us, event | category | flops | bytes accessed | tf_op | source)
XLA Modules:
  0.0 172.1 jit_solution(17710834893021719364)
XLA Ops:
  0.6 168.6 %shard_map.93 = bf16[4,128,2048]{2,1,0:T(8,128)(2,1)} custom-call(bf16[128,2048]{1,0:T(8,128)(2,1)} %q_ref.1, bf16[128,2048]{1,0:T(8,128)(2,1)} %k_ref.1, bf16[128,2048]{1,0:T(8,128)(2,1)} %v_ref.1, bf16[128,2048]{1,0:T(8,128)(2,1)} %g_ref.1, s32[1,512]{1,0:T(1,128)} %bitcast.10, s32[1,512]{1,0:T(1,128)} %bitcast.11), custom_call_target="tpu_custom_call" | custom-call | tf_op jit(solution)/shard_map/pallas_call | solution.py:653
  169.2 2.9 %slice_bitcast_fusion = (bf16[128,2048]{1,0:T(8,128)(2,1)}, bf16[128,2048]{1,0:T(8,128)(2,1)}, bf16[128,2048]{1,0:T(8,128)(2,1)}, bf16[128,2048]{1,0:T(8,128)(2,1)}) fusion(bf16[4,128,2048]{2,1,0:T(8,128)(2,1)} %shard_map.93), kind=kLoop, calls=%fused_computation | loop fusion | bytes 4194304 | tf_op jit(solution)/shard_map/squeeze | solution.py:670

commit v5 on v4

--- a/solution.py
+++ b/solution.py
@@ -555,12 +555,13 @@
     pack_and_send(keys_flow, 2, PARTS)
     to_heads(1, range(2, 4))
     from_heads(1)
-    pack_and_send(query_flows[0], 0, PARTS)
+    pack_and_send(query_flows[0], 0, 3)
     keys_arrive()
     mean_line()
-    pack_and_send(query_flows[1], 0, 2)
+    pack_and_send(query_flows[0], 3, PARTS)
+    pack_and_send(query_flows[1], 0, 1)
     mean_plane()
-    pack_and_send(query_flows[1], 2, PARTS)
+    pack_and_send(query_flows[1], 1, PARTS)
     mean_take()
     receive(query_flows[0], asked)
     attend(0)

time: 172 us -> 166 us (0.965)
  Pallas kernels: 169 us -> 161 us
    pallas_call x1, Pallas kernels: 169 us -> 161 us  [per_device(): pl.pallas_call(functools.partial(kernel, seq_count, head_count, plane, ca...]
where the time goes in v5:
time: 166 us; the launch traced here: 165 us
  Pallas kernels  161 us (97%)
  local copies, waits for them, and re-layouts  2.88 us (2%)
    pallas_call x1, Pallas kernels, per_device(): pl.pallas_call(functools.partial(kernel, seq_count, head_count, plane, ca...  161 us

profile of v5, /device:TPU:1, one launch (start us, length us, event | category | flops | bytes accessed | tf_op | source)
XLA Modules:
  0.0 164.9 jit_solution(16035733093109439344)
XLA Ops:
  0.6 161.4 %shard_map.93 = bf16[4,128,2048]{2,1,0:T(8,128)(2,1)} custom-call(bf16[128,2048]{1,0:T(8,128)(2,1)} %q_ref.1, bf16[128,2048]{1,0:T(8,128)(2,1)} %k_ref.1, bf16[128,2048]{1,0:T(8,128)(2,1)} %v_ref.1, bf16[128,2048]{1,0:T(8,128)(2,1)} %g_ref.1, s32[1,512]{1,0:T(1,128)} %bitcast.10, s32[1,512]{1,0:T(1,128)} %bitcast.11), custom_call_target="tpu_custom_call" | custom-call | tf_op jit(solution)/shard_map/pallas_call | solution.py:654
  162.0 2.9 %slice_bitcast_fusion = (bf16[128,2048]{1,0:T(8,128)(2,1)}, bf16[128,2048]{1,0:T(8,128)(2,1)}, bf16[128,2048]{1,0:T(8,128)(2,1)}, bf16[128,2048]{1,0:T(8,128)(2,1)}) fusion(bf16[4,128,2048]{2,1,0:T(8,128)(2,1)} %shard_map.93), kind=kLoop, calls=%fused_computation | loop fusion | bytes 4194304 | tf_op jit(solution)/shard_map/squeeze | solution.py:671

commit v6 on v5

--- a/solution.py
+++ b/solution.py
@@ -546,7 +546,9 @@
                     {"head": other},
                 )
 
-            place[...] = home_out[chunk, i, my_rows, :]
+            pltpu.make_async_copy(
+                home_out.at[chunk, i, my_rows], place, home_own.at[chunk]
+            ).start()
 
     from_heads(0)
     pl.semaphore_wait(plane_ready, plane - 1)
@@ -584,6 +586,8 @@
             wait_bytes(home_out.at[chunk, :, others], out_recv.at[chunk])
             wait_bytes(home_out.at[chunk, :, others], out_send.at[chunk])
             wait_bytes(home.at[chunk, :, others], home_send.at[chunk])
+    for chunk in range(2):
+        wait_bytes(home_out.at[chunk, :, pl.ds(0, rows)], home_own.at[chunk])
     for stream in (keys_flow, *query_flows, *answer_flows, grads_flow):
         wait_sent(stream)
     wait_bytes(mean_line_bytes, line_send)
@@ -650,12 +654,11 @@
     scratch += [by_chunk] * 3 + [by_flow, by_part] * 2 + [by_chunk] * 3 + [dma] * 8
     scratch += [pltpu.SemaphoreType.REGULAR]
     in_hbm = pl.BlockSpec(memory_space=pltpu.HBM)
-    in_vmem = pl.BlockSpec(memory_space=pltpu.VMEM)
     staged = pl.pallas_call(
         functools.partial(kernel, seq_count, head_count, plane, capacity),
         out_shape=jax.ShapeDtypeStruct((4, rows, full), BF16),
         in_specs=[in_hbm] * 6,
-        out_specs=in_vmem,
+        out_specs=in_hbm,
         scratch_shapes=scratch,
         compiler_params=pltpu.CompilerParams(
             collective_id=0, has_side_effects=True, vmem_limit_bytes=63 * 1024 * 1024

time: 166 us -> 164 us (0.988)
  no operation moved by 1% of the time
where the time goes in v6:
time: 164 us
  Pallas kernels  161 us (98%)
  local copies, waits for them, and re-layouts  2.88 us (2%)
    pallas_call x1, Pallas kernels, per_device(): pl.pallas_call(functools.partial(kernel, seq_count, head_count, plane, ca...  161 us

profile of v6, /device:TPU:1, one launch (start us, length us, event | category | flops | bytes accessed | tf_op | source)
XLA Modules:
  0.0 164.4 jit_solution(9100697406478757807)
XLA Ops:
  0.6 160.9 %shard_map.93 = bf16[4,128,2048]{2,1,0:T(8,128)(2,1)} custom-call(bf16[128,2048]{1,0:T(8,128)(2,1)} %q_ref.1, bf16[128,2048]{1,0:T(8,128)(2,1)} %k_ref.1, bf16[128,2048]{1,0:T(8,128)(2,1)} %v_ref.1, bf16[128,2048]{1,0:T(8,128)(2,1)} %g_ref.1, s32[1,512]{1,0:T(1,128)} %bitcast.10, s32[1,512]{1,0:T(1,128)} %bitcast.11), custom_call_target="tpu_custom_call" | custom-call | tf_op jit(solution)/shard_map/pallas_call | solution.py:657
  161.5 2.9 %slice_bitcast_fusion = (bf16[128,2048]{1,0:T(8,128)(2,1)}, bf16[128,2048]{1,0:T(8,128)(2,1)}, bf16[128,2048]{1,0:T(8,128)(2,1)}, bf16[128,2048]{1,0:T(8,128)(2,1)}) fusion(bf16[4,128,2048]{2,1,0:T(8,128)(2,1)} %shard_map.93), kind=kLoop, calls=%fused_computation | loop fusion | bytes 4194304 | tf_op jit(solution)/shard_map/squeeze | solution.py:674
